TPU v7x, 32 devices: a whole 2x2x4 slice. The times are simulated.
32 devices in a mesh: az: 8 (over z, x), rad: 4 (over y, core).
Axes of the slice: x: 2, y: 2, z: 4, core: 2. Of those that a mesh axis runs over, the one named last changes fastest.
Arguments:
- fields: float32 [8, 64, 256, 128], P(None, 'rad', 'az'), as said below
- offsets: int32 [64], replicated, may hold values from 0 to 255
- boundary_shift: int32 [1], replicated, may hold values from 0 to 255
Outputs:
- advanced: float32 [8, 64, 256, 128], P(None, 'rad', 'az')
Inputs may be any that keep to these rules, and one draw needn't show every extreme that they name: Each cell of fields is a conserved state whose density and implied pressure lie between 0.5 and 2; velocities stay under 1.8 and field components under 0.9 in magnitude.
All inputs are finite; a program needn't handle non-finite values.
Results may differ from a plain program's by a relative error of at most 0.0003.
Values sent between devices are 32-bit elements; how exact they have to be, the bound alone decides.
A program may use at most 192 MiB of HBM per device.

v0:
```python
import jax
import jax.numpy as jnp
from jax import lax
from jax.sharding import PartitionSpec as P

GAMMA_RATIO = 5.0 / 3.0
CFL_NUMBER = 0.4
OMEGA_RATE = 1.0
SHEAR_RATE = 1.5


def passed_along(array, axis, by):
    devices = lax.axis_size(axis)
    return lax.ppermute(array, axis, [(i, (i + by) % devices) for i in range(devices)])


def padded(block, sides, width):
    for axis, dim in sides:
        count = lax.axis_size(axis)
        forward = [(i, i + 1) for i in range(count - 1)]
        forward.append((count - 1, 0))
        backward = [(target, source) for source, target in forward]
        low = lax.ppermute(
            lax.slice_in_dim(block, block.shape[dim] - width, None, axis=dim), axis, forward
        )
        high = lax.ppermute(lax.slice_in_dim(block, 0, width, axis=dim), axis, backward)
        block = jnp.concatenate([low, block, high], axis=dim)
    return block


def primitive(state):
    density = state[0]
    inverse = 1.0 / density
    speed_x = state[1] * inverse
    speed_y = state[2] * inverse
    speed_z = state[3] * inverse
    kinetic = 0.5 * density * (speed_x * speed_x + speed_y * speed_y + speed_z * speed_z)
    magnetic = 0.5 * (state[5] * state[5] + state[6] * state[6] + state[7] * state[7])
    pressure = (GAMMA_RATIO - 1.0) * (state[4] - kinetic - magnetic)
    return (density, speed_x, speed_y, speed_z, pressure, state[5], state[6], state[7])


def fast_speed(density, pressure, normal_field, field_sq):
    sound = (GAMMA_RATIO * pressure + field_sq) / density
    spread = jnp.maximum(
        sound * sound
        - 4.0 * GAMMA_RATIO * pressure * normal_field * normal_field / (density * density),
        0.0,
    )
    return jnp.sqrt(0.5 * (sound + jnp.sqrt(spread)))


def cell_speed(primitives):
    field_sq = (
        primitives[5] * primitives[5]
        + primitives[6] * primitives[6]
        + primitives[7] * primitives[7]
    )
    total = jnp.abs(primitives[1]) + fast_speed(
        primitives[0], primitives[4], primitives[5], field_sq
    )
    total = (
        total
        + jnp.abs(primitives[2])
        + fast_speed(primitives[0], primitives[4], primitives[6], field_sq)
    )
    total = (
        total
        + jnp.abs(primitives[3])
        + fast_speed(primitives[0], primitives[4], primitives[7], field_sq)
    )
    return total


def minmod(first_diff, second_diff):
    return (
        0.5
        * (jnp.sign(first_diff) + jnp.sign(second_diff))
        * jnp.minimum(jnp.abs(first_diff), jnp.abs(second_diff))
    )


def take_range(values, start_at, stop_at, along):
    return lax.slice_in_dim(values, start_at, stop_at, axis=along)


def side_terms(values, normal_field):
    density, normal_speed, trans_speed, other_speed, pressure = (
        values[0],
        values[1],
        values[2],
        values[3],
        values[4],
    )
    trans_field, other_field = (values[6], values[7])
    field_sq = normal_field * normal_field + trans_field * trans_field + other_field * other_field
    total_press = pressure + 0.5 * field_sq
    energy = (
        pressure / (GAMMA_RATIO - 1.0)
        + 0.5
        * density
        * (normal_speed * normal_speed + trans_speed * trans_speed + other_speed * other_speed)
        + 0.5 * field_sq
    )
    field_work = normal_speed * normal_field + trans_speed * trans_field + other_speed * other_field
    conserved = (
        density,
        density * normal_speed,
        density * trans_speed,
        density * other_speed,
        energy,
        normal_field,
        trans_field,
        other_field,
    )
    fluxes = (
        density * normal_speed,
        density * normal_speed * normal_speed + total_press - normal_field * normal_field,
        density * normal_speed * trans_speed - normal_field * trans_field,
        density * normal_speed * other_speed - normal_field * other_field,
        (energy + total_press) * normal_speed - normal_field * field_work,
        jnp.zeros_like(density),
        trans_field * normal_speed - normal_field * trans_speed,
        other_field * normal_speed - normal_field * other_speed,
    )
    signal = fast_speed(density, pressure, normal_field, field_sq)
    return (conserved, fluxes, total_press, energy, field_work, signal)


def star_state(values, energy, total_press, field_work, normal_field, outer, middle, star_press):
    density, normal_speed, trans_speed, other_speed = (values[0], values[1], values[2], values[3])
    trans_field, other_field = (values[6], values[7])
    relative = outer - normal_speed
    distance = outer - middle
    star_density = density * relative / distance
    product = density * relative * distance
    divisor = jnp.maximum(product - normal_field * normal_field, 0.5 * product)
    trans_star = trans_speed - normal_field * trans_field * (middle - normal_speed) / divisor
    other_star = other_speed - normal_field * other_field * (middle - normal_speed) / divisor
    factor = (density * relative * relative - normal_field * normal_field) / divisor
    trans_bstar = trans_field * factor
    other_bstar = other_field * factor
    star_work = middle * normal_field + trans_star * trans_bstar + other_star * other_bstar
    star_energy = (
        relative * energy
        - total_press * normal_speed
        + star_press * middle
        + normal_field * (field_work - star_work)
    ) / distance
    return (star_density, trans_star, other_star, trans_bstar, other_bstar, star_work, star_energy)


def hlld_flux(left_values, right_values):
    normal_field = 0.5 * (left_values[5] + right_values[5])
    cons_left, flux_left, press_left, energy_left, work_left, signal_left = side_terms(
        left_values, normal_field
    )
    cons_right, flux_right, press_right, energy_right, work_right, signal_right = side_terms(
        right_values, normal_field
    )
    fastest = jnp.maximum(signal_left, signal_right)
    lower = jnp.minimum(left_values[1], right_values[1]) - fastest
    upper = jnp.maximum(left_values[1], right_values[1]) + fastest
    mass_left = left_values[0] * (lower - left_values[1])
    mass_right = right_values[0] * (upper - right_values[1])
    guess = (
        mass_right * right_values[1] - mass_left * left_values[1] - press_right + press_left
    ) / (mass_right - mass_left)
    margin = 0.1 * (upper - lower)
    middle = jnp.clip(guess, lower + margin, upper - margin)
    star_press = press_left + mass_left * (middle - left_values[1])
    dens_left, trans_left, other_left, tfield_left, ofield_left, swork_left, senergy_left = (
        star_state(
            left_values, energy_left, press_left, work_left, normal_field, lower, middle, star_press
        )
    )
    dens_right, trans_right, other_right, tfield_right, ofield_right, swork_right, senergy_right = (
        star_state(
            right_values,
            energy_right,
            press_right,
            work_right,
            normal_field,
            upper,
            middle,
            star_press,
        )
    )
    root_left = jnp.sqrt(dens_left)
    root_right = jnp.sqrt(dens_right)
    sign_field = jnp.sign(normal_field)
    root_sum = root_left + root_right
    trans_double = (
        root_left * trans_left
        + root_right * trans_right
        + (tfield_right - tfield_left) * sign_field
    ) / root_sum
    other_double = (
        root_left * other_left
        + root_right * other_right
        + (ofield_right - ofield_left) * sign_field
    ) / root_sum
    tfield_double = (
        root_left * tfield_right
        + root_right * tfield_left
        + root_left * root_right * (trans_right - trans_left) * sign_field
    ) / root_sum
    ofield_double = (
        root_left * ofield_right
        + root_right * ofield_left
        + root_left * root_right * (other_right - other_left) * sign_field
    ) / root_sum
    double_work = (
        middle * normal_field + trans_double * tfield_double + other_double * ofield_double
    )
    denergy_left = senergy_left - root_left * (swork_left - double_work) * sign_field
    denergy_right = senergy_right + root_right * (swork_right - double_work) * sign_field
    inner_left = middle - jnp.abs(normal_field) / root_left
    inner_right = middle + jnp.abs(normal_field) / root_right
    star_cons_left = (
        dens_left,
        dens_left * middle,
        dens_left * trans_left,
        dens_left * other_left,
        senergy_left,
        normal_field,
        tfield_left,
        ofield_left,
    )
    star_cons_right = (
        dens_right,
        dens_right * middle,
        dens_right * trans_right,
        dens_right * other_right,
        senergy_right,
        normal_field,
        tfield_right,
        ofield_right,
    )
    double_cons_left = (
        dens_left,
        dens_left * middle,
        dens_left * trans_double,
        dens_left * other_double,
        denergy_left,
        normal_field,
        tfield_double,
        ofield_double,
    )
    double_cons_right = (
        dens_right,
        dens_right * middle,
        dens_right * trans_double,
        dens_right * other_double,
        denergy_right,
        normal_field,
        tfield_double,
        ofield_double,
    )
    outcome = []
    for component in range(8):
        star_left = flux_left[component] + lower * (
            star_cons_left[component] - cons_left[component]
        )
        double_left = star_left + inner_left * (
            double_cons_left[component] - star_cons_left[component]
        )
        star_right = flux_right[component] + upper * (
            star_cons_right[component] - cons_right[component]
        )
        double_right = star_right + inner_right * (
            double_cons_right[component] - star_cons_right[component]
        )
        chosen = jnp.where(
            lower > 0,
            flux_left[component],
            jnp.where(
                inner_left > 0,
                star_left,
                jnp.where(
                    middle > 0,
                    double_left,
                    jnp.where(
                        inner_right > 0,
                        double_right,
                        jnp.where(upper > 0, star_right, flux_right[component]),
                    ),
                ),
            ),
        )
        outcome.append(chosen)
    outcome[5] = jnp.zeros_like(outcome[0])
    return outcome


def direction_divergence(primitives, along, normal_order):
    mapping = (
        0,
        normal_order[0],
        normal_order[1],
        normal_order[2],
        4,
        normal_order[0] + 4,
        normal_order[1] + 4,
        normal_order[2] + 4,
    )
    left_faces = []
    right_faces = []
    for component in range(8):
        values = primitives[mapping[component]]
        length = values.shape[along]
        cell_count = length - 4
        differences = take_range(values, 1, length, along) - take_range(
            values, 0, length - 1, along
        )
        slopes = minmod(
            take_range(differences, 0, length - 2, along),
            take_range(differences, 1, length - 1, along),
        )
        centres = take_range(values, 1, length - 1, along)
        left_faces.append(
            take_range(centres, 0, cell_count + 1, along)
            + 0.5 * take_range(slopes, 0, cell_count + 1, along)
        )
        right_faces.append(
            take_range(centres, 1, cell_count + 2, along)
            - 0.5 * take_range(slopes, 1, cell_count + 2, along)
        )
    face_fluxes = hlld_flux(left_faces, right_faces)
    result = [None] * 8
    for component in range(8):
        face_values = face_fluxes[component]
        length = face_values.shape[along]
        result[mapping[component]] = take_range(face_values, 1, length, along) - take_range(
            face_values, 0, length - 1, along
        )
    return result


def advance(radial_padded, azimuthal_padded, remapped, time_step):
    radial_div = direction_divergence(primitive(radial_padded), 0, (1, 2, 3))
    azimuthal_div = direction_divergence(primitive(azimuthal_padded), 1, (2, 3, 1))
    vertical_padded = jnp.concatenate([remapped[..., -2:], remapped, remapped[..., :2]], axis=3)
    vertical_div = direction_divergence(primitive(vertical_padded), 2, (3, 1, 2))
    gains = [
        0.0,
        2.0 * OMEGA_RATE * remapped[2],
        -(2.0 - SHEAR_RATE) * OMEGA_RATE * remapped[1],
        0.0,
        SHEAR_RATE
        * OMEGA_RATE
        * (remapped[1] * remapped[2] / remapped[0] - remapped[5] * remapped[6]),
        0.0,
        -SHEAR_RATE * OMEGA_RATE * remapped[5],
        0.0,
    ]
    outcome = []
    for component in range(8):
        change = radial_div[component] + azimuthal_div[component] + vertical_div[component]
        outcome.append(remapped[component] - time_step * change + time_step * gains[component])
    return jnp.stack(outcome)


def rotate(blocks, shifts, loop_cells):
    cell_width = blocks.shape[2]
    amount = jnp.mod(shifts, loop_cells)
    whole_part = amount // cell_width
    remainder = amount - whole_part * cell_width
    for bit_index in range(lax.axis_size("az").bit_length() - 1):
        shifted = passed_along(blocks, "az", 1 << bit_index)
        chosen = jnp.bitwise_and(jnp.right_shift(whole_part, bit_index), 1) == 1
        blocks = jnp.where(chosen[None, :, None, None], shifted, blocks)
    before = passed_along(blocks, "az", 1)
    joined = jnp.concatenate([before, blocks], axis=2)
    positions = cell_width + jnp.arange(cell_width, dtype=jnp.int32)[None, :] - remainder[:, None]
    return jnp.take_along_axis(joined, positions[None, :, :, None], axis=2)


def radial_rim(blocks):
    return padded(blocks, (("rad", 1),), 2)


def local(fields, offsets, boundary_shift):
    row_count = fields.shape[1]
    cell_width = fields.shape[2]
    loop_cells = cell_width * lax.axis_size("az")
    radial_cells = row_count * lax.axis_size("rad")
    local_peak = jnp.max(cell_speed(primitive(fields)))
    global_peak = lax.pmax(local_peak, ("az", "rad"))
    time_step = CFL_NUMBER / global_peak
    radial_index = lax.axis_index("rad")
    first_row = radial_index * row_count
    shear_cells = boundary_shift[0]
    extended = radial_rim(fields)
    global_rows = first_row - 2 + jnp.arange(row_count + 4, dtype=jnp.int32)
    source_rows = jnp.mod(global_rows, radial_cells)
    boundary_extra = jnp.where(global_rows < 0, shear_cells, 0) - jnp.where(
        global_rows >= radial_cells, shear_cells, 0
    )
    radial_padded = rotate(extended, jnp.take(offsets, source_rows) + boundary_extra, loop_cells)
    remapped = radial_padded[:, 2 : row_count + 2]
    azimuthal_padded = padded(remapped, (("az", 2),), 2)
    return advance(radial_padded, azimuthal_padded, remapped, time_step)


def solution(mesh):
    in_specs = (P(None, "rad", "az", None), P(), P())
    out_specs = P(None, "rad", "az", None)
    return jax.shard_map(local, mesh=mesh, in_specs=in_specs, out_specs=out_specs, check_vma=False)
```

profile of v0, /device:TPU:0, one launch (start us, length us, event | category | flops | bytes accessed | tf_op | source)
XLA Modules:
  0.0 419.3 jit_solution(10878337128948392769)
XLA Ops:
  0.0 1.2 fusion.408
  1.4 0.5 collective-permute-start
  2.1 2.0 collective-permute-start.1
  4.1 3.8 collective-permute-done
  7.9 0.7 constant_dynamic-update-slice_fusion.2
  8.6 3.0 constant_dynamic-update-slice_fusion.1
  11.6 0.7 constant_dynamic-update-slice_fusion
  12.4 3.0 collective-permute-start.2
  16.0 0.7 gather_fusion
  16.8 59.4 %collective-permute-done.2 = f32[8,20,32,128]{3,0,2,1:T(8,128)} collective-permute-done((f32[8,20,32,128]{3,0,2,1:T(8,128)}, f32[8,20,32,128]{3,0,2,1:T(8,128)}, u32[]{:S(2)}, u32[]{:S(2)}) %collective-permute-start.2) | collective-permute-done | bytes 2621472 | tf_op jit(solution)/shard_map/ppermute | solution.py:14
  76.2 2.9 broadcast_select_fusion
  79.2 60.7 %collective-permute-done.3 = f32[8,20,32,128]{3,0,2,1:T(8,128)S(1)} collective-permute-done((f32[8,20,32,128]{3,0,2,1:T(8,128)S(1)}, f32[8,20,32,128]{3,0,2,1:T(8,128)S(1)}, u32[]{:S(2)}, u32[]{:S(2)}) %collective-permute-start.3) | collective-permute-done | bytes 2621472 | tf_op jit(solution)/shard_map/ppermute | solution.py:14
  139.9 0.4 broadcast_select_fusion.1
  140.4 113.4 %collective-permute-done.4 = f32[8,20,32,128]{3,0,2,1:T(8,128)S(1)} collective-permute-done((f32[8,20,32,128]{3,0,2,1:T(8,128)S(1)}, f32[8,20,32,128]{3,0,2,1:T(8,128)S(1)}, u32[]{:S(2)}, u32[]{:S(2)}) %collective-permute-start.4) | collective-permute-done | bytes 2621472 | tf_op jit(solution)/shard_map/ppermute | solution.py:14
  253.7 1.9 broadcast_select_fusion.2
  255.6 1.5 add_reduce_fusion
  257.0 91.2 %pmax.7 = f32[]{:T(128)} all-reduce(f32[]{:T(128)} %add_reduce_fusion), channel_id=1, replica_groups=mesh['az'=8,'rad'=4] {'az','rad'}, use_global_device_ids=true, to_apply=%region_1.0 | all-reduce | flops 1 | bytes 8 | tf_op jit(solution)/shard_map/pmax | solution.py:389
  349.2 5.4 %pad_maximum_fusion = f32[8,20,64,128]{3,0,2,1:T(8,128)} fusion(f32[8,20,32,128]{3,0,2,1:T(8,128)} %broadcast_select_fusion.2, f32[8,20,32,128]{3,0,2,1:T(8,128)} %collective-permute-done.5), kind=kLoop, calls=%fused_computation.2 | loop fusion | flops 1310720 | bytes 10485760 | tf_op jit(solution)/shard_map/concatenate | solution.py:374
  354.5 9.1 %gather_fusion.1 = f32[640,8,128]{2,1,0:T(8,128)} fusion(f32[8,20,64,128]{3,0,2,1:T(8,128)} %pad_maximum_fusion, s32[640]{0:T(1024)S(1)} %reshape.452), kind=kCustom, calls=%fused_computation.1 | custom fusion | bytes 5248000 | tf_op jit(solution)/shard_map/jit(take_along_axis)/gather | solution.py:376
  363.6 2.3 fusion
  366.2 0.3 fusion.133
  366.7 0.7 fusion.407
  367.5 1.7 pad_maximum_fusion.1
  369.2 0.2 slice_bitcast_fusion.6
  369.4 0.7 fusion.41
  370.1 0.3 slice_subtract_fusion.2
  370.4 0.4 minimum_multiply_fusion.2
  370.8 0.4 minimum_multiply_fusion.3
  371.2 0.3 slice_subtract_fusion.4
  371.6 0.4 minimum_multiply_fusion.4
  371.9 0.4 minimum_multiply_fusion.5
  372.3 0.5 slice_subtract_fusion.6
  372.9 0.4 minimum_multiply_fusion.6
  373.2 0.4 minimum_multiply_fusion.7
  373.6 0.3 slice_subtract_fusion
  374.0 0.4 minimum_multiply_fusion
  374.3 0.4 minimum_multiply_fusion.1
  374.7 4.7 %select_select_fusion = (f32[16,32,129]{2,1,0:T(8,128)S(1)}, f32[16,32,129]{2,1,0:T(8,128)S(1)}, f32[16,32,129]{2,1,0:T(8,128)S(1)}, f32[16,32,129]{2,1,0:T(8,12...) fusion(f32[16,32,130]{2,1,0:T(8,128)S(1)} %minimum_multiply_fus, ...), kind=kLoop, calls=%fused_computation.90 | loop fusion | flops 10897920 | bytes 11096064 | tf_op jit(solution)/shard_map/jit(_where)/select_n | solution.py:274
  379.4 2.8 select_select_fusion.2
  382.2 4.3 %fusion.17 = f32[16,32,129]{2,1,0:T(8,128)S(1)} fusion(f32[16,32,129]{2,1,0:T(8,128)S(1)} %get-tuple-element.42, f32[16,32,129]{2,1,0:T(8,128)S(1)} %get-tuple-element.45, f32[16,32,129]{2,1,0:T(8,128)S(1)} %get-tuple-element.39, f32[16,32,129]{2,1,0:T(8,128)S(1)} %get-tuple-element.38, f32[16,32,129]{2,1,0:T(8,128)S(1)} %get-tuple-element.46, ...), kind=kLoop, calls=%fused_computation.30 | loop fusion | flops 13671936 | bytes 5812224 | tf_op jit(solution)/shard_map/jit(_where)/select_n | solution.py:274
  386.5 3.0 select_select_fusion.1
  389.5 2.3 collective-permute-start.6
  391.8 2.4 collective-permute-start.7
  394.9 0.2 minimum_multiply_fusion.16
  395.2 0.2 minimum_multiply_fusion.18
  395.4 2.6 select_select_fusion.10
  398.0 1.5 select_select_fusion.11
  399.5 2.2 fusion.192
  401.7 1.4 select_select_fusion.12
  403.1 0.4 pad_maximum_fusion.2
  403.9 0.2 minimum_multiply_fusion.10
  404.2 0.2 minimum_multiply_fusion.11
  404.5 0.2 minimum_multiply_fusion.12
  404.7 0.2 minimum_multiply_fusion.13
  405.1 0.2 minimum_multiply_fusion.14
  405.3 0.2 minimum_multiply_fusion.15
  405.6 0.2 minimum_multiply_fusion.8
  406.1 3.1 select_select_fusion.5
  409.2 1.7 select_select_fusion.7
  410.9 2.8 fusion.102
  413.8 1.8 select_select_fusion.6
  416.3 0.3 fusion.318
  417.0 1.3 copy-done.3
  418.3 0.8 fusion.300
  (46 shorter events, 3.6 us)
Async XLA Ops:
  0.0 16.0 %copy-start = (s32[64]{0:T(128)S(1)}, s32[64]{0:T(128)}, u32[]{:S(2)}) copy-start(s32[64]{0:T(128)} %param.4) | copy-start | bytes 772
  0.0 8.6 %copy-start.2 = (f32[8,16,32,128]{3,2,1,0:T(8,128)S(1)}, f32[8,16,32,128]{3,2,1,0:T(8,128)}, u32[]{:S(2)}) copy-start(f32[8,16,32,128]{3,2,1,0:T(8,128)} %param.3) | copy-start | bytes 6291460
  1.4 6.5 %collective-permute-start = (f32[8,2,32,128]{3,0,2,1:T(8,128)S(1)}, f32[8,2,32,128]{3,0,2,1:T(8,128)S(1)}, u32[]{:S(2)}, u32[]{:S(2)}) collective-permute-start(f32[8,2,32,128]{3,0,2,1:T(8,128)S(1)} %copy.12), channel_id=1, source_target_pairs={{0,1},{1,2},{2,3},{3,0},{4,5},{5,6},{6,7},{7,4},{8,9},{9,10},{10,1... | collective-permute-start | bytes 786440 | tf_op jit(solution)/shard_map/ppermute | solution.py:23
  2.1 9.6 %collective-permute-start.1 = (f32[8,2,32,128]{3,0,2,1:T(8,128)S(1)}, f32[8,2,32,128]{3,0,2,1:T(8,128)S(1)}, u32[]{:S(2)}, u32[]{:S(2)}) collective-permute-start(f32[8,2,32,128]{3,0,2,1:T(8,128)S(1)} %copy.13), channel_id=1, source_target_pairs={{1,0},{2,1},{3,2},{0,3},{5,4},{6,5},{7,6},{4,7},{9,8},{10,9},{11,1... | collective-permute-start | bytes 786440 | tf_op jit(solution)/shard_map/ppermute | solution.py:26
  12.4 63.8 %collective-permute-start.2 = (f32[8,20,32,128]{3,0,2,1:T(8,128)}, f32[8,20,32,128]{3,0,2,1:T(8,128)}, u32[]{:S(2)}, u32[]{:S(2)}) collective-permute-start(f32[8,20,32,128]{3,0,2,1:T(8,128)} %constant_dynamic-update-slice_fusion), channel_id=1, source_target_pairs={{0,4},{4,8},{8,12},{12,16},{16,20},{20,24},{24,28},{28,0},{1,5},{5... | collective-permute-start | bytes 7864328 | tf_op jit(solution)/shard_map/ppermute | solution.py:14
  79.1 60.7 %collective-permute-start.3 = (f32[8,20,32,128]{3,0,2,1:T(8,128)S(1)}, f32[8,20,32,128]{3,0,2,1:T(8,128)S(1)}, u32[]{:S(2)}, u32[]{:S(2)}) collective-permute-start(f32[8,20,32,128]{3,0,2,1:T(8,128)S(1)} %broadcast_select_fusion), channel_id=1, source_target_pairs={{0,8},{4,12},{8,16},{12,20},{16,24},{20,28},{24,0},{28,4},{1,9},{5... | collective-permute-start | bytes 7864328 | tf_op jit(solution)/shard_map/ppermute | solution.py:14
  140.3 113.4 %collective-permute-start.4 = (f32[8,20,32,128]{3,0,2,1:T(8,128)S(1)}, f32[8,20,32,128]{3,0,2,1:T(8,128)S(1)}, u32[]{:S(2)}, u32[]{:S(2)}) collective-permute-start(f32[8,20,32,128]{3,0,2,1:T(8,128)S(1)} %broadcast_select_fusion.1), channel_id=1, source_target_pairs={{0,16},{4,20},{8,24},{12,28},{16,0},{20,4},{24,8},{28,12},{1,17},{... | collective-permute-start | bytes 7864328 | tf_op jit(solution)/shard_map/ppermute | solution.py:14
  255.6 93.6 %collective-permute-start.5 = (f32[8,20,32,128]{3,0,2,1:T(8,128)}, f32[8,20,32,128]{3,0,2,1:T(8,128)}, u32[]{:S(2)}, u32[]{:S(2)}) collective-permute-start(f32[8,20,32,128]{3,0,2,1:T(8,128)} %broadcast_select_fusion.2), channel_id=1, source_target_pairs={{0,4},{4,8},{8,12},{12,16},{16,20},{20,24},{24,28},{28,0},{1,5},{5... | collective-permute-start | bytes 7864328 | tf_op jit(solution)/shard_map/ppermute | solution.py:14
  389.5 13.6 %collective-permute-start.6 = (f32[8,16,2,128]{3,2,1,0:T(2,128)S(1)}, f32[8,16,2,128]{3,2,1,0:T(2,128)S(1)}, u32[]{:S(2)}, u32[]{:S(2)}) collective-permute-start(f32[8,16,2,128]{3,2,1,0:T(2,128)S(1)} %get-tuple-element.84), channel_id=1, source_target_pairs={{0,4},{4,8},{8,12},{12,16},{16,20},{20,24},{24,28},{28,0},{1,5},{5... | collective-permute-start | bytes 393224 | tf_op jit(solution)/shard_map/ppermute | solution.py:23
  391.8 11.3 %collective-permute-start.7 = (f32[8,16,2,128]{3,2,1,0:T(2,128)S(1)}, f32[8,16,2,128]{3,2,1,0:T(2,128)S(1)}, u32[]{:S(2)}, u32[]{:S(2)}) collective-permute-start(f32[8,16,2,128]{3,2,1,0:T(2,128)S(1)} %get-tuple-element.85), channel_id=1, source_target_pairs={{4,0},{8,4},{12,8},{16,12},{20,16},{24,20},{28,24},{0,28},{5,1},{9... | collective-permute-start | bytes 393224 | tf_op jit(solution)/shard_map/ppermute | solution.py:26
  416.3 2.8 copy-start.1
  416.9 1.3 copy-start.3
where the time goes:
time: 424 us; the launch traced here: 419 us
  waiting for transfers between devices  237 us (56%)
  blocking collectives  91.2 us (22%)
  other arithmetic  59.8 us (14%)
  local copies, waits for them, and re-layouts  18.5 us (4%)
  starting transfers between devices  10.4 us (2%)
    ppermute x4, waiting for transfers between devices, passed_along(): lax.ppermute(array, axis, [(i, (i + by) % devices) for i in range(devices)])  233 us
    pmax x1, blocking collectives, local(): global_peak = lax.pmax(local_peak, ('az', 'rad'))  91.2 us
    select_n x12, other arithmetic, hlld_flux(): jnp.where(lower > 0, flux_left[component], jnp.where(inner_left > 0, star...  31.9 us
    gather x2, local copies, waits for them, and re-layouts, rotate(): return jnp.take_along_axis(joined, positions[None, :, :, None], axis=2)  9.16 us
  transfers between devices with their start and end apart: 8, of which 4 were waited for; matrix products, arithmetic and copies ran while one was open for 4% of the time, Pallas kernels for 0%

commit v1 on v0

--- a/solution.py
+++ b/solution.py
@@ -7,25 +7,6 @@
 CFL_NUMBER = 0.4
 OMEGA_RATE = 1.0
 SHEAR_RATE = 1.5
-
-
-def passed_along(array, axis, by):
-    devices = lax.axis_size(axis)
-    return lax.ppermute(array, axis, [(i, (i + by) % devices) for i in range(devices)])
-
-
-def padded(block, sides, width):
-    for axis, dim in sides:
-        count = lax.axis_size(axis)
-        forward = [(i, i + 1) for i in range(count - 1)]
-        forward.append((count - 1, 0))
-        backward = [(target, source) for source, target in forward]
-        low = lax.ppermute(
-            lax.slice_in_dim(block, block.shape[dim] - width, None, axis=dim), axis, forward
-        )
-        high = lax.ppermute(lax.slice_in_dim(block, 0, width, axis=dim), axis, backward)
-        block = jnp.concatenate([low, block, high], axis=dim)
-    return block
 
 
 def primitive(state):
@@ -361,45 +342,50 @@
     return jnp.stack(outcome)
 
 
-def rotate(blocks, shifts, loop_cells):
-    cell_width = blocks.shape[2]
-    amount = jnp.mod(shifts, loop_cells)
-    whole_part = amount // cell_width
-    remainder = amount - whole_part * cell_width
-    for bit_index in range(lax.axis_size("az").bit_length() - 1):
-        shifted = passed_along(blocks, "az", 1 << bit_index)
-        chosen = jnp.bitwise_and(jnp.right_shift(whole_part, bit_index), 1) == 1
-        blocks = jnp.where(chosen[None, :, None, None], shifted, blocks)
-    before = passed_along(blocks, "az", 1)
-    joined = jnp.concatenate([before, blocks], axis=2)
-    positions = cell_width + jnp.arange(cell_width, dtype=jnp.int32)[None, :] - remainder[:, None]
-    return jnp.take_along_axis(joined, positions[None, :, :, None], axis=2)
-
-
-def radial_rim(blocks):
-    return padded(blocks, (("rad", 1),), 2)
-
-
 def local(fields, offsets, boundary_shift):
-    row_count = fields.shape[1]
-    cell_width = fields.shape[2]
-    loop_cells = cell_width * lax.axis_size("az")
-    radial_cells = row_count * lax.axis_size("rad")
-    local_peak = jnp.max(cell_speed(primitive(fields)))
-    global_peak = lax.pmax(local_peak, ("az", "rad"))
-    time_step = CFL_NUMBER / global_peak
+    parts, rows, cells, depth = fields.shape
+    azimuth_devices = lax.axis_size("az")
+    radial_devices = lax.axis_size("rad")
+    loop_cells = cells * azimuth_devices
+    radial_cells = rows * radial_devices
+    time_step = CFL_NUMBER / lax.pmax(jnp.max(cell_speed(primitive(fields))), ("az", "rad"))
     radial_index = lax.axis_index("rad")
-    first_row = radial_index * row_count
+    lowest = radial_index == 0
+    highest = radial_index == radial_devices - 1
     shear_cells = boundary_shift[0]
-    extended = radial_rim(fields)
-    global_rows = first_row - 2 + jnp.arange(row_count + 4, dtype=jnp.int32)
-    source_rows = jnp.mod(global_rows, radial_cells)
-    boundary_extra = jnp.where(global_rows < 0, shear_cells, 0) - jnp.where(
-        global_rows >= radial_cells, shear_cells, 0
-    )
-    radial_padded = rotate(extended, jnp.take(offsets, source_rows) + boundary_extra, loop_cells)
-    remapped = radial_padded[:, 2 : row_count + 2]
-    azimuthal_padded = padded(remapped, (("az", 2),), 2)
+    ghost = lax.ppermute(
+        jnp.where(lowest, fields[:, :2], fields[:, rows - 2 :]),
+        "rad",
+        [(0, radial_devices - 1), (radial_devices - 1, 0)],
+    )
+    units = jnp.concatenate([fields, ghost], axis=1).reshape(parts * (rows + 2), cells, depth)
+    share = units.shape[0] // azimuth_devices
+    rings = lax.all_to_all(units, "az", 0, 1, tiled=True)
+    slot = jnp.mod(lax.axis_index("az") * share + jnp.arange(share, dtype=jnp.int32), rows + 2)
+    ghost_row = jnp.where(lowest, radial_cells - 2, 0) + slot - rows
+    row = jnp.where(slot < rows, radial_index * rows + slot, ghost_row)
+    extra = jnp.where(slot < rows, 0, jnp.where(lowest, shear_cells, -shear_cells))
+    shift = jnp.take(offsets, row) + extra
+    width = cells + 4
+    columns = (
+        jnp.arange(azimuth_devices, dtype=jnp.int32)[:, None] * cells
+        - 2
+        + jnp.arange(width, dtype=jnp.int32)[None, :]
+    ).reshape(-1)
+    positions = jnp.mod(columns[None, :] - shift[:, None], loop_cells)
+    windows = jnp.take_along_axis(rings, positions[:, :, None], axis=1)
+    landed = lax.all_to_all(windows, "az", 1, 0, tiled=True)
+    landed = landed.reshape(parts, rows + 2, width, depth)
+    azimuthal_padded = landed[:, :rows]
+    forward = [(i, (i + 1) % radial_devices) for i in range(radial_devices)]
+    backward = [(target, source) for source, target in forward]
+    remapped = azimuthal_padded[:, :, 2 : cells + 2]
+    spare = landed[:, rows:, 2 : cells + 2]
+    low = lax.ppermute(remapped[:, rows - 2 :], "rad", forward)
+    high = lax.ppermute(remapped[:, :2], "rad", backward)
+    low = jnp.where(lowest, spare, low)
+    high = jnp.where(highest, spare, high)
+    radial_padded = jnp.concatenate([low, remapped, high], axis=1)
     return advance(radial_padded, azimuthal_padded, remapped, time_step)
 
 

time: 424 us -> 310 us (0.73)
  waiting for transfers between devices: 237 us -> 57.1 us
  local copies, waits for them, and re-layouts: 18.5 us -> 73.1 us
  blocking collectives: 91.2 us -> 98.3 us
  starting transfers between devices: 10.4 us -> 15.6 us
    ppermute x8 -> x3, waiting for transfers between devices: 237 us -> 11.9 us  [the longest x1 5.07 us: local(): high = lax.ppermute(remapped[:, :2], 'rad', backward)]
    gather x3, local copies, waits for them, and re-layouts: 9.85 us -> 63.8 us  [the longest x2 63.1 us: local(): windows = jnp.take_along_axis(rings, positions[:, :, None], axis=1)]
    all_to_all x0 -> x2, waiting for transfers between devices: none -> 45.1 us  [the longest x1 45.1 us: local(): rings = lax.all_to_all(units, 'az', 0, 1, tiled=True)]
    all_to_all x0 -> x2, starting transfers between devices: none -> 10.2 us  [the longest x1 6.58 us: local(): rings = lax.all_to_all(units, 'az', 0, 1, tiled=True)]
    pmax x1, blocking collectives: 91.2 us -> 98.3 us  [local(): lax.pmax(jnp.max(cell_speed(primitive(fields))), ('az', 'rad'))]
    ppermute x8 -> x3, starting transfers between devices: 10.4 us -> 5.38 us  [the longest x1 4.31 us: local(): lax.ppermute(jnp.where(lowest, fields[:, :2], fields[:, rows - 2:]), 'rad...]
  transfers between devices with their start and end apart: 8 -> 5, of which waited for: 4 -> 4; matrix products, arithmetic and copies ran while one was open for 4% -> 2% of each run, Pallas kernels for 0% -> 0%
where the time goes in v1:
time: 310 us; the launch traced here: 305 us
  blocking collectives  98.3 us (32%)
  local copies, waits for them, and re-layouts  73.1 us (24%)
  other arithmetic  59 us (19%)
  waiting for transfers between devices  57.1 us (18%)
  starting transfers between devices  15.6 us (5%)
    pmax x1, blocking collectives, local(): lax.pmax(jnp.max(cell_speed(primitive(fields))), ('az', 'rad'))  98.3 us
    gather x2, local copies, waits for them, and re-layouts, local(): windows = jnp.take_along_axis(rings, positions[:, :, None], axis=1)  63.1 us
    all_to_all x1, waiting for transfers between devices, local(): rings = lax.all_to_all(units, 'az', 0, 1, tiled=True)  45.1 us
    select_n x12, other arithmetic, hlld_flux(): jnp.where(lower > 0, flux_left[component], jnp.where(inner_left > 0, star...  32 us
    all_to_all x1, starting transfers between devices, local(): rings = lax.all_to_all(units, 'az', 0, 1, tiled=True)  6.58 us
  transfers between devices with their start and end apart: 5, of which 4 were waited for; matrix products, arithmetic and copies ran while one was open for 2% of the time, Pallas kernels for 0%

profile of v1, /device:TPU:0, one launch (start us, length us, event | category | flops | bytes accessed | tf_op | source)
XLA Modules:
  0.0 305.3 jit_solution(251923077642100299)
XLA Ops:
  0.0 1.1 slice_select_fusion
  1.1 4.3 %collective-permute-start = (f32[8,2,32,128]{3,2,1,0:T(8,128)S(1)}, f32[8,2,32,128]{3,2,1,0:T(8,128)S(1)}, u32[]{:S(2)}, u32[]{:S(2)}) collective-permute-start(f32[8,2,32,128]{3,2,1,0:T(8,128)S(1)} %slice_select_fusion), channel_id=1, source_target_pairs={{0,3},{3,0},{4,7},{7,4},{8,11},{11,8},{12,15},{15,12},{16,19},{19,... | collective-permute-start | bytes 786440 | tf_op jit(solution)/shard_map/ppermute | solution.py:356
  5.4 4.0 %collective-permute-done = f32[8,2,32,128]{3,2,1,0:T(8,128)S(1)} collective-permute-done((f32[8,2,32,128]{3,2,1,0:T(8,128)S(1)}, f32[8,2,32,128]{3,2,1,0:T(8,128)S(1)}, u32[]{:S(2)}, u32[]{:S(2)}) %collective-permute-start) | collective-permute-done | bytes 262176 | tf_op jit(solution)/shard_map/ppermute | solution.py:356
  9.4 3.3 %pad_maximum_fusion.2 = f32[8,18,32,128]{3,2,1,0:T(8,128)} fusion(f32[8,2,32,128]{3,2,1,0:T(8,128)S(1)} %collective-permute-done, f32[8,16,32,128]{3,2,1,0:T(8,128)} %param.3), kind=kLoop, calls=%fused_computation.6 | loop fusion | flops 589824 | bytes 4718592 | tf_op jit(solution)/shard_map/concatenate | solution.py:361
  12.7 6.6 %all-to-all-start = ((f32[144,32,128]{2,1,0:T(8,128)}), f32[144,32,128]{2,1,0:T(8,128)S(1)}, u32[]{:S(2)}, u32[]{:S(2)}) async-start(f32[144,32,128]{2,1,0:T(8,128)} %bitcast.343), calls=%async_computation | async-start | bytes 4718592 | tf_op jit(solution)/shard_map/all_to_all | solution.py:363
  20.2 0.7 gather_fusion
  21.3 45.1 %all-to-all-done = f32[144,32,128]{2,1,0:T(8,128)S(1)} async-done(((f32[144,32,128]{2,1,0:T(8,128)}), f32[144,32,128]{2,1,0:T(8,128)S(1)}, u32[]{:S(2)}, u32[]{:S(2)}) %all-to-all-start) | async-done | bytes 2359328 | tf_op jit(solution)/shard_map/all_to_all | solution.py:363
  66.4 1.4 copy-done.2
  67.8 1.9 copy.26
  69.7 63.0 %gather_fusion.1 = f32[5184,128]{1,0:T(8,128)} fusion(f32[18,256,128]{2,1,0:T(8,128)S(1)} %bitcast.334, s32[5184]{0:T(1024)S(1)} %reshape.396), kind=kCustom, calls=%fused_computation.1 | custom fusion | bytes 5349888 | tf_op jit(solution)/shard_map/jit(take_along_axis)/gather | solution.py:376
  132.7 5.1 %copy_select_fusion = f32[18,288,128]{2,0,1:T(8,128)} fusion(f32[18,288,128]{2,1,0:T(8,128)} %bitcast.341, pred[18,288]{0,1:T(8,128)(4,1)S(1)} %compare_and_fusion), kind=kLoop, calls=%fused_computation.3 | loop fusion | flops 663552 | bytes 5313600 | tf_op jit(solution)/shard_map/jit(take_along_axis)/select_n | solution.py:376
  137.8 3.7 %all-to-all-start.1 = ((f32[18,288,128]{2,0,1:T(8,128)}), f32[18,288,128]{2,0,1:T(8,128)S(1)}, u32[]{:S(2)}, u32[]{:S(2)}) async-start(f32[18,288,128]{2,0,1:T(8,128)} %copy_select_fusion), calls=%async_computation.1 | async-start | bytes 7077888 | tf_op jit(solution)/shard_map/all_to_all | solution.py:377
  141.4 3.0 add_reduce_fusion
  144.4 98.3 %pmax.7 = f32[]{:T(128)} all-reduce(f32[]{:T(128)} %add_reduce_fusion), channel_id=1, replica_groups=mesh['az'=8,'rad'=4] {'az','rad'}, use_global_device_ids=true, to_apply=%region_1.0 | all-reduce | flops 1 | bytes 8 | tf_op jit(solution)/shard_map/pmax | solution.py:351
  243.4 0.4 fusion.398
  244.4 0.2 minimum_multiply_fusion.11
  244.7 0.2 minimum_multiply_fusion.10
  245.2 0.2 minimum_multiply_fusion.12
  245.5 0.2 minimum_multiply_fusion.13
  245.7 0.7 fusion.129
  247.5 3.1 %select_select_fusion.5 = (f32[16,33,128]{2,1,0:T(8,128)S(1)}, f32[16,33,128]{2,1,0:T(8,128)S(1)}, f32[16,33,128]{2,1,0:T(8,128)S(1)}, f32[16,33,128]{2,1,0:T(8,...) fusion(f32[16,34,128]{2,1,0:T(8,128)S(1)} %minimum_multiply_fus, ...), kind=kLoop, calls=%fused_computation.276 | loop fusion | flops 11151360 | bytes 11354112 | tf_op jit(solution)/shard_map/jit(_where)/select_n | solution.py:255
  250.7 1.7 select_select_fusion.7
  252.4 2.8 fusion.101
  255.2 1.8 select_select_fusion.6
  257.1 0.7 fusion.400
  257.8 0.6 copy.55
  258.5 0.6 copy.65
  259.1 0.6 copy.66
  259.7 1.7 pad_maximum_fusion
  261.4 0.2 slice_bitcast_fusion.6
  261.7 0.7 fusion.40
  262.4 0.3 slice_subtract_fusion.2
  262.7 0.4 minimum_multiply_fusion.2
  263.1 0.4 minimum_multiply_fusion.3
  263.5 0.3 slice_subtract_fusion.4
  263.8 0.4 minimum_multiply_fusion.4
  264.2 0.4 minimum_multiply_fusion.5
  264.6 0.3 slice_subtract_fusion.6
  264.9 0.4 minimum_multiply_fusion.6
  265.3 0.4 minimum_multiply_fusion.7
  265.7 0.3 slice_subtract_fusion
  266.0 0.4 minimum_multiply_fusion
  266.4 0.4 minimum_multiply_fusion.1
  266.8 4.9 %select_select_fusion = (f32[16,32,129]{2,1,0:T(8,128)S(1)}, f32[16,32,129]{2,1,0:T(8,128)S(1)}, f32[16,32,129]{2,1,0:T(8,128)S(1)}, f32[16,32,129]{2,1,0:T(8,12...) fusion(f32[16,32,130]{2,1,0:T(8,128)S(1)} %minimum_multiply_fus, ...), kind=kLoop, calls=%fused_computation.87 | loop fusion | flops 10897920 | bytes 11096064 | tf_op jit(solution)/shard_map/jit(_where)/select_n | solution.py:255
  271.7 2.8 select_select_fusion.2
  274.4 4.3 %fusion.16 = f32[16,32,129]{2,1,0:T(8,128)S(1)} fusion(f32[16,32,129]{2,1,0:T(8,128)S(1)} %get-tuple-element.42, f32[16,32,129]{2,1,0:T(8,128)S(1)} %get-tuple-element.45, f32[16,32,129]{2,1,0:T(8,128)S(1)} %get-tuple-element.39, f32[16,32,129]{2,1,0:T(8,128)S(1)} %get-tuple-element.38, f32[16,32,129]{2,1,0:T(8,128)S(1)} %get-tuple-element.46, ...), kind=kLoop, calls=%fused_computation.27 | loop fusion | flops 13671936 | bytes 5812224 | tf_op jit(solution)/shard_map/jit(_where)/select_n | solution.py:255
  278.7 3.0 select_select_fusion.1
  281.8 1.1 collective-permute-start.2
  282.9 0.5 copy.162
  283.6 5.1 %collective-permute-done.2 = f32[8,2,32,128]{3,2,1,0:T(8,128)S(1)} collective-permute-done((f32[8,2,32,128]{3,2,1,0:T(8,128)S(1)}, f32[8,2,32,128]{3,2,1,0:T(8,128)S(1)}, u32[]{:S(2)}, u32[]{:S(2)}) %collective-permute-start.2) | collective-permute-done | bytes 262176 | tf_op jit(solution)/shard_map/ppermute | solution.py:385
  288.7 2.8 collective-permute-done.1
  291.6 0.2 pad_maximum_fusion.1
  292.0 0.3 fusion.126
  293.0 0.2 minimum_multiply_fusion.16
  293.2 0.2 minimum_multiply_fusion.18
  293.5 2.4 select_select_fusion.10
  295.9 1.4 select_select_fusion.12
  297.3 2.2 fusion.191
  299.5 1.5 select_select_fusion.11
  301.2 0.3 fusion.338
  301.5 0.3 fusion.331
  301.9 0.6 fusion.317
  302.9 1.3 copy-done.3
  304.3 0.8 fusion.299
  (46 shorter events, 4.3 us)
Async XLA Ops:
  0.0 20.1 %copy-start = (s32[64]{0:T(128)S(1)}, s32[64]{0:T(128)}, u32[]{:S(2)}) copy-start(s32[64]{0:T(128)} %param.4) | copy-start | bytes 772
  1.1 8.4 %collective-permute-start = (f32[8,2,32,128]{3,2,1,0:T(8,128)S(1)}, f32[8,2,32,128]{3,2,1,0:T(8,128)S(1)}, u32[]{:S(2)}, u32[]{:S(2)}) collective-permute-start(f32[8,2,32,128]{3,2,1,0:T(8,128)S(1)} %slice_select_fusion), channel_id=1, source_target_pairs={{0,3},{3,0},{4,7},{7,4},{8,11},{11,8},{12,15},{15,12},{16,19},{19,... | collective-permute-start | bytes 786440 | tf_op jit(solution)/shard_map/ppermute | solution.py:356
  12.7 53.7 %all-to-all-start = ((f32[144,32,128]{2,1,0:T(8,128)}), f32[144,32,128]{2,1,0:T(8,128)S(1)}, u32[]{:S(2)}, u32[]{:S(2)}) async-start(f32[144,32,128]{2,1,0:T(8,128)} %bitcast.343), calls=%async_computation | async-start | bytes 4718592 | tf_op jit(solution)/shard_map/all_to_all | solution.py:363
  66.4 1.4 copy-start.2
  137.8 105.7 %all-to-all-start.1 = ((f32[18,288,128]{2,0,1:T(8,128)}), f32[18,288,128]{2,0,1:T(8,128)S(1)}, u32[]{:S(2)}, u32[]{:S(2)}) async-start(f32[18,288,128]{2,0,1:T(8,128)} %copy_select_fusion), calls=%async_computation.1 | async-start | bytes 7077888 | tf_op jit(solution)/shard_map/all_to_all | solution.py:377
  281.8 6.8 %collective-permute-start.2 = (f32[8,2,32,128]{3,2,1,0:T(8,128)S(1)}, f32[8,2,32,128]{3,2,1,0:T(8,128)S(1)}, u32[]{:S(2)}, u32[]{:S(2)}) collective-permute-start(f32[8,2,32,128]{3,2,1,0:T(8,128)S(1)} %copy.56), channel_id=1, source_target_pairs={{1,0},{2,1},{3,2},{0,3},{5,4},{6,5},{7,6},{4,7},{9,8},{10,9},{11,1... | collective-permute-start | bytes 786440 | tf_op jit(solution)/shard_map/ppermute | solution.py:385
  282.9 8.6 %collective-permute-start.1 = (f32[8,2,32,128]{3,2,1,0:T(8,128)S(1)}, f32[8,2,32,128]{3,2,1,0:T(8,128)S(1)}, u32[]{:S(2)}, u32[]{:S(2)}) collective-permute-start(f32[8,2,32,128]{3,2,1,0:T(8,128)S(1)} %copy.54), channel_id=1, source_target_pairs={{0,1},{1,2},{2,3},{3,0},{4,5},{5,6},{6,7},{7,4},{8,9},{9,10},{10,1... | collective-permute-start | bytes 786440 | tf_op jit(solution)/shard_map/ppermute | solution.py:384
  302.5 2.6 copy-start.1
  302.9 1.3 copy-start.3

commit v2 on v1

v2 whole, which is shorter than its diff:
```python
import functools

import jax
import jax.numpy as jnp
from jax import lax
from jax.experimental import pallas as pl
from jax.experimental.pallas import tpu as pltpu
from jax.sharding import PartitionSpec as P

GAMMA_RATIO = 5.0 / 3.0
CFL_NUMBER = 0.4
OMEGA_RATE = 1.0
SHEAR_RATE = 1.5


def primitive(state):
    density = state[0]
    inverse = 1.0 / density
    speed_x = state[1] * inverse
    speed_y = state[2] * inverse
    speed_z = state[3] * inverse
    kinetic = 0.5 * density * (speed_x * speed_x + speed_y * speed_y + speed_z * speed_z)
    magnetic = 0.5 * (state[5] * state[5] + state[6] * state[6] + state[7] * state[7])
    pressure = (GAMMA_RATIO - 1.0) * (state[4] - kinetic - magnetic)
    return (density, speed_x, speed_y, speed_z, pressure, state[5], state[6], state[7])


def fast_speed(density, pressure, normal_field, field_sq):
    sound = (GAMMA_RATIO * pressure + field_sq) / density
    spread = jnp.maximum(
        sound * sound
        - 4.0 * GAMMA_RATIO * pressure * normal_field * normal_field / (density * density),
        0.0,
    )
    return jnp.sqrt(0.5 * (sound + jnp.sqrt(spread)))


def cell_speed(primitives):
    field_sq = (
        primitives[5] * primitives[5]
        + primitives[6] * primitives[6]
        + primitives[7] * primitives[7]
    )
    total = jnp.abs(primitives[1]) + fast_speed(
        primitives[0], primitives[4], primitives[5], field_sq
    )
    total = (
        total
        + jnp.abs(primitives[2])
        + fast_speed(primitives[0], primitives[4], primitives[6], field_sq)
    )
    total = (
        total
        + jnp.abs(primitives[3])
        + fast_speed(primitives[0], primitives[4], primitives[7], field_sq)
    )
    return total


ADIABATIC = 1.0 / (GAMMA_RATIO - 1.0)
ORDERS = ((1, 2, 3), (2, 3, 1), (3, 1, 2))
MARGIN = 8


def inverse_of(values):
    return 1.0 / values


def half_slope(first_diff, second_diff):
    return 0.5 * (
        jnp.maximum(jnp.minimum(first_diff, second_diff), 0.0)
        + jnp.minimum(jnp.maximum(first_diff, second_diff), 0.0)
    )


def half_square_speed(density, pressure, normal_sq, field_sq):
    inverse = inverse_of(density)
    sound = (GAMMA_RATIO * pressure + field_sq) * inverse
    spread = sound * sound - (4.0 * GAMMA_RATIO) * pressure * normal_sq * (inverse * inverse)
    return 0.5 * (sound + jnp.sqrt(jnp.maximum(spread, 0.0)))


def star_part(values, mass, gap, outer, middle, bn, bn_sq):
    distance = outer - middle
    inverse = inverse_of(distance)
    density = mass * inverse
    product = mass * distance
    divisor = inverse_of(jnp.maximum(product - bn_sq, 0.5 * product))
    turn = bn * (middle - values[1]) * divisor
    factor = (mass * gap - bn_sq) * divisor
    root_inverse = lax.rsqrt(density)
    return (
        density,
        values[2] - values[6] * turn,
        values[3] - values[7] * turn,
        values[6] * factor,
        values[7] * factor,
        inverse,
        density * root_inverse,
        root_inverse,
    )


def face_flux(left, right):
    bn = 0.5 * (left[5] + right[5])
    bn_sq = bn * bn
    sq_left = bn_sq + left[6] * left[6] + left[7] * left[7]
    sq_right = bn_sq + right[6] * right[6] + right[7] * right[7]
    fastest = jnp.sqrt(
        jnp.maximum(
            half_square_speed(left[0], left[4], bn_sq, sq_left),
            half_square_speed(right[0], right[4], bn_sq, sq_right),
        )
    )
    lower = jnp.minimum(left[1], right[1]) - fastest
    upper = jnp.maximum(left[1], right[1]) + fastest
    gap_left = lower - left[1]
    gap_right = upper - right[1]
    mass_left = left[0] * gap_left
    mass_right = right[0] * gap_right
    press_left = left[4] + 0.5 * sq_left
    press_right = right[4] + 0.5 * sq_right
    guess = (
        mass_right * right[1] - mass_left * left[1] - press_right + press_left
    ) * inverse_of(mass_right - mass_left)
    margin = 0.1 * (upper - lower)
    middle = jnp.minimum(jnp.maximum(guess, lower + margin), upper - margin)
    star_press = press_left + mass_left * (middle - left[1])
    star_left = star_part(left, mass_left, gap_left, lower, middle, bn, bn_sq)
    star_right = star_part(right, mass_right, gap_right, upper, middle, bn, bn_sq)
    sign = jnp.where(bn > 0.0, 1.0, jnp.where(bn < 0.0, -1.0, 0.0))
    root_left, root_right = star_left[6], star_right[6]
    share = inverse_of(root_left + root_right)
    share_left = root_left * share
    share_right = root_right * share
    kick = sign * share
    cross = root_left * share_right * sign
    v_double = (
        share_left * star_left[1]
        + share_right * star_right[1]
        + (star_right[3] - star_left[3]) * kick
    )
    w_double = (
        share_left * star_left[2]
        + share_right * star_right[2]
        + (star_right[4] - star_left[4]) * kick
    )
    bt_double = (
        share_left * star_right[3]
        + share_right * star_left[3]
        + (star_right[1] - star_left[1]) * cross
    )
    bw_double = (
        share_left * star_right[4]
        + share_right * star_left[4]
        + (star_right[2] - star_left[2]) * cross
    )
    on_left = middle > 0.0

    def pick(first, second):
        return jnp.where(on_left, first, second)

    rho, u, v, w, p, bt, bw = (pick(left[c], right[c]) for c in (0, 1, 2, 3, 4, 6, 7))
    pt = pick(press_left, press_right)
    outer = pick(lower, upper)
    gap = pick(gap_left, gap_right)
    rho_s, v_s, w_s, bt_s, bw_s, inv_s, root_s, root_inv = (
        pick(a, b) for a, b in zip(star_left, star_right)
    )
    energy = (ADIABATIC - 1.0) * p + pt + 0.5 * rho * (u * u + v * v + w * w)
    work = u * bn + v * bt + w * bw
    middle_work = middle * bn
    work_s = middle_work + v_s * bt_s + w_s * bw_s
    work_d = middle_work + v_double * bt_double + w_double * bw_double
    energy_s = (gap * energy - pt * u + star_press * middle + bn * (work - work_s)) * inv_s
    side = pick(sign, -sign)
    energy_step = side * root_s * (work_d - work_s)
    alfven = jnp.abs(bn) * root_inv
    inner = middle - pick(alfven, -alfven)
    outer_on = outer > 0.0
    inner_on = inner > 0.0
    first = jnp.where(
        on_left, jnp.where(outer_on, 0.0, outer), jnp.where(inner_on | outer_on, outer, 0.0)
    )
    second = jnp.where(
        on_left, jnp.where(outer_on | inner_on, 0.0, inner), jnp.where(inner_on, inner, 0.0)
    )
    momentum = rho * u
    second_mass = second * rho_s
    return (
        momentum + first * (rho_s - rho),
        momentum * u + pt - bn_sq + first * (rho_s * middle - momentum),
        momentum * v - bn * bt + first * (rho_s * v_s - rho * v) + second_mass * (v_double - v_s),
        momentum * w - bn * bw + first * (rho_s * w_s - rho * w) + second_mass * (w_double - w_s),
        (energy + pt) * u - bn * work + first * (energy_s - energy) + second * energy_step,
        bt * u - bn * v + first * (bt_s - bt) + second * (bt_double - bt_s),
        bw * u - bn * w + first * (bw_s - bw) + second * (bw_double - bw_s),
    )


def targets(order):
    return (0, order[0], order[1], order[2], 4, order[1] + 4, order[2] + 4)


def sources(order):
    return (0, order[0], order[1], order[2], 4, order[0] + 4, order[1] + 4, order[2] + 4)


def faces_between(before, here, after, beyond):
    middle_diff = after - here
    return (
        here + half_slope(here - before, middle_diff),
        after - half_slope(middle_diff, beyond - after),
    )


def flux_between(read, order):
    pairs = [faces_between(*read(c)) for c in sources(order)]
    return face_flux([pair[0] for pair in pairs], [pair[1] for pair in pairs])


def flux_kernel(landed, low, high, step, out, prims, radial_flux, ring_flux):
    rows, cells = out.shape[1], out.shape[2]
    depth = out.shape[3]
    chunks = cells // 8
    dt = step[0]

    def fill(i, _):
        values = primitive([landed[f, i] for f in range(8)])
        for f in range(8):
            prims[f, i + 2, MARGIN - 2 : MARGIN + cells + 2] = values[f]
        return 0

    lax.fori_loop(0, rows, fill, 0)
    for g in range(2):
        for ref, row in ((low, g), (high, rows + 2 + g)):
            values = primitive([ref[f, g] for f in range(8)])
            for f in range(8):
                prims[f, row, MARGIN : MARGIN + cells] = values[f]

    def radial(row, q):
        columns = slice(MARGIN + 8 * q, MARGIN + 8 * q + 8)
        return flux_between(
            lambda c: [prims[c, row + near, columns] for near in (-1, 0, 1, 2)], ORDERS[0]
        )

    for q in range(chunks):
        for c, value in enumerate(radial(1, q)):
            radial_flux[c, 8 * q : 8 * q + 8] = value

    def advance_row(i, _):
        row = i + 2
        for q in range(chunks + 1):
            begin = MARGIN - 1 + 8 * q
            fluxes = flux_between(
                lambda c: [
                    prims[c, row, begin + near : begin + near + 8] for near in (-1, 0, 1, 2)
                ],
                ORDERS[1],
            )
            for c, value in enumerate(fluxes):
                ring_flux[c, 8 * q : 8 * q + 8] = value
        for q in range(chunks):
            inside = slice(8 * q, 8 * q + 8)
            columns = slice(MARGIN + 8 * q, MARGIN + 8 * q + 8)
            change = [None] * 8

            def gather(order, values):
                for c, value in zip(targets(order), values):
                    change[c] = value if change[c] is None else change[c] + value

            upper = radial(row, q)
            gather(ORDERS[0], [value - radial_flux[c, inside] for c, value in enumerate(upper)])
            for c, value in enumerate(upper):
                radial_flux[c, inside] = value
            gather(
                ORDERS[1],
                [ring_flux[c, 8 * q + 1 : 8 * q + 9] - ring_flux[c, inside] for c in range(7)],
            )
            lefts, rights = [], []
            for c in sources(ORDERS[2]):
                here = prims[c, row, columns]
                diff = pltpu.roll(here, depth - 1, 1) - here
                slope = half_slope(pltpu.roll(diff, 1, 1), diff)
                lefts.append(here + slope)
                rights.append(pltpu.roll(here - slope, depth - 1, 1))
            above = face_flux(lefts, rights)
            gather(ORDERS[2], [value - pltpu.roll(value, 1, 1) for value in above])
            state = [landed[f, i, 8 * q + 2 : 8 * q + 10] for f in range(8)]
            speed_x = prims[1, row, columns]
            gains = {
                1: (2.0 * OMEGA_RATE) * state[2],
                2: (-(2.0 - SHEAR_RATE) * OMEGA_RATE) * state[1],
                4: (SHEAR_RATE * OMEGA_RATE) * (speed_x * state[2] - state[5] * state[6]),
                6: (-SHEAR_RATE * OMEGA_RATE) * state[5],
            }
            for f in range(8):
                total = gains[f] - change[f] if f in gains else -change[f]
                out[f, i, inside] = state[f] + dt * total
        return 0

    lax.fori_loop(0, rows, advance_row, 0)


def advanced(landed, low, high, time_step, rows, cells):
    parts, depth = landed.shape[0], landed.shape[3]
    vmem = pl.BlockSpec(memory_space=pltpu.VMEM)
    return pl.pallas_call(
        flux_kernel,
        out_shape=jax.ShapeDtypeStruct((parts, rows, cells, depth), jnp.float32),
        in_specs=[vmem, vmem, vmem, pl.BlockSpec(memory_space=pltpu.SMEM)],
        out_specs=vmem,
        scratch_shapes=[
            pltpu.VMEM((parts, rows + 4, cells + 3 * MARGIN, depth), jnp.float32),
            pltpu.VMEM((7, cells, depth), jnp.float32),
            pltpu.VMEM((7, cells + 8, depth), jnp.float32),
        ],
        compiler_params=pltpu.CompilerParams(vmem_limit_bytes=40 * 1024 * 1024),
        name="advance",
    )(landed, low, high, time_step.reshape(1))


def turn_kernel(count, shifts, ring, out, doubled):
    loop_cells = ring.shape[1]
    cells = loop_cells // count
    width = out.shape[2]
    doubled[:loop_cells] = ring[0]
    doubled[loop_cells : loop_cells + width] = ring[0, :width]
    shift = shifts[pl.program_id(0)]
    for t in range(count):
        start = lax.rem(t * cells - 2 - shift + 4 * loop_cells, loop_cells)
        out[0, t] = doubled[pl.ds(start, width)]


def turned(rings, shift, count):
    share, loop_cells, depth = rings.shape
    width = loop_cells // count + 4
    return pl.pallas_call(
        functools.partial(turn_kernel, count),
        out_shape=jax.ShapeDtypeStruct((share, count, width, depth), jnp.float32),
        grid_spec=pltpu.PrefetchScalarGridSpec(
            num_scalar_prefetch=1,
            grid=(share,),
            in_specs=[pl.BlockSpec((1, loop_cells, depth), lambda u, s: (u, 0, 0))],
            out_specs=pl.BlockSpec((1, count, width, depth), lambda u, s: (u, 0, 0, 0)),
            scratch_shapes=[pltpu.VMEM((loop_cells + width + 4, depth), jnp.float32)],
        ),
        name="turn",
    )(shift, rings)


def local(fields, offsets, boundary_shift):
    parts, rows, cells, depth = fields.shape
    azimuth_devices = lax.axis_size("az")
    radial_devices = lax.axis_size("rad")
    loop_cells = cells * azimuth_devices
    radial_cells = rows * radial_devices
    time_step = CFL_NUMBER / lax.pmax(jnp.max(cell_speed(primitive(fields))), ("az", "rad"))
    radial_index = lax.axis_index("rad")
    lowest = radial_index == 0
    highest = radial_index == radial_devices - 1
    shear_cells = boundary_shift[0]
    ghost = lax.ppermute(
        jnp.where(lowest, fields[:, :2], fields[:, rows - 2 :]),
        "rad",
        [(0, radial_devices - 1), (radial_devices - 1, 0)],
    )
    units = jnp.concatenate([fields, ghost], axis=1).reshape(parts * (rows + 2), cells, depth)
    share = units.shape[0] // azimuth_devices
    rings = lax.all_to_all(units, "az", 0, 1, tiled=True)
    slot = jnp.mod(lax.axis_index("az") * share + jnp.arange(share, dtype=jnp.int32), rows + 2)
    ghost_row = jnp.where(lowest, radial_cells - 2, 0) + slot - rows
    row = jnp.where(slot < rows, radial_index * rows + slot, ghost_row)
    extra = jnp.where(slot < rows, 0, jnp.where(lowest, shear_cells, -shear_cells))
    shift = jnp.take(offsets, row) + extra
    windows = turned(rings, jnp.mod(shift, loop_cells), azimuth_devices)
    landed = lax.all_to_all(windows, "az", 1, 0, tiled=True)
    landed = landed.reshape(parts, rows + 2, cells + 4, depth)
    forward = [(i, (i + 1) % radial_devices) for i in range(radial_devices)]
    backward = [(target, source) for source, target in forward]
    spare = landed[:, rows:, 2 : cells + 2]
    low = lax.ppermute(landed[:, rows - 2 : rows, 2 : cells + 2], "rad", forward)
    high = lax.ppermute(landed[:, :2, 2 : cells + 2], "rad", backward)
    low = jnp.where(lowest, spare, low)
    high = jnp.where(highest, spare, high)
    return advanced(landed, low, high, time_step, rows, cells)


def solution(mesh):
    in_specs = (P(None, "rad", "az", None), P(), P())
    out_specs = P(None, "rad", "az", None)
    return jax.shard_map(local, mesh=mesh, in_specs=in_specs, out_specs=out_specs, check_vma=False)
```

time: 310 us -> 222 us (0.72); the launches traced: 305 us -> 221 us
  local copies, waits for them, and re-layouts: 73.1 us -> 4.46 us
  other arithmetic: 59 us -> 8.96 us
  Pallas kernels: 0 us -> 29.6 us
  blocking collectives: 98.3 us -> 107 us
  waiting for transfers between devices: 57.1 us -> 53.1 us
    all_to_all x0 -> x1, blocking collectives: none -> 68.5 us  [local(): landed = lax.all_to_all(windows, 'az', 1, 0, tiled=True)]
    gather x2 -> x0, local copies, waits for them, and re-layouts: 63.1 us -> none  [local(): windows = jnp.take_along_axis(rings, positions[:, :, None], axis=1)]
    pmax x1, blocking collectives: 98.3 us -> 38.6 us  [local(): lax.pmax(jnp.max(cell_speed(primitive(fields))), ('az', 'rad'))]
    select_n x13 -> x2, other arithmetic: 37.1 us -> 1.57 us  [the longest x1 1.03 us: local(): high = jnp.where(highest, spare, high)]
    pallas_call x0 -> x2, Pallas kernels: none -> 29.6 us  [the longest x1 18.3 us: advanced(): pl.pallas_call(flux_kernel, out_shape=jax.ShapeDtypeStruct((parts, rows,...]
    mul x25 -> x0, other arithmetic: 7.63 us -> none  [the longest x22 5.91 us: minmod(): 0.5 * (jnp.sign(first_diff) + jnp.sign(second_diff))]
    unnamed x13 -> x2, local copies, waits for them, and re-layouts: 4.67 us -> 0.01 us
    ppermute x2, starting transfers between devices: 1.06 us -> 5.4 us  [the longest x1 3.15 us: local(): high = lax.ppermute(landed[:, :2, 2:cells + 2], 'rad', backward)]
  transfers between devices with their start and end apart: 5 -> 4, of which waited for: 4 -> 3; matrix products, arithmetic and copies ran while one was open for 2% -> 2% of each run, Pallas kernels for 0% -> 0%
where the time goes in v2:
time: 222 us; the launch traced here: 221 us
  blocking collectives  107 us (48%)
  waiting for transfers between devices  53.1 us (24%)
  Pallas kernels  29.6 us (13%)
  starting transfers between devices  16.3 us (7%)
  other arithmetic  8.96 us (4%)
  local copies, waits for them, and re-layouts  4.46 us (2%)
    all_to_all x1, blocking collectives, local(): landed = lax.all_to_all(windows, 'az', 1, 0, tiled=True)  68.5 us
    all_to_all x1, waiting for transfers between devices, local(): rings = lax.all_to_all(units, 'az', 0, 1, tiled=True)  45.1 us
    pmax x1, blocking collectives, local(): lax.pmax(jnp.max(cell_speed(primitive(fields))), ('az', 'rad'))  38.6 us
    pallas_call x1, Pallas kernels, advanced(): pl.pallas_call(flux_kernel, out_shape=jax.ShapeDtypeStruct((parts, rows,...  18.3 us
    pallas_call x1, Pallas kernels, turned(): pl.pallas_call(functools.partial(turn_kernel, count), out_shape=jax.Shape...  11.3 us
    all_to_all x1, starting transfers between devices, local(): rings = lax.all_to_all(units, 'az', 0, 1, tiled=True)  6.58 us
  transfers between devices with their start and end apart: 4, of which 3 were waited for; matrix products, arithmetic and copies ran while one was open for 2% of the time, Pallas kernels for 0%

profile of v2, /device:TPU:0, one launch (start us, length us, event | category | flops | bytes accessed | tf_op | source)
XLA Modules:
  0.0 221.0 jit_solution(977058984137776359)
XLA Ops:
  0.0 0.0 copy-start
  0.0 1.1 slice_select_fusion
  1.1 4.3 %collective-permute-start = (f32[8,2,32,128]{3,2,1,0:T(8,128)S(1)}, f32[8,2,32,128]{3,2,1,0:T(8,128)S(1)}, u32[]{:S(2)}, u32[]{:S(2)}) collective-permute-start(f32[8,2,32,128]{3,2,1,0:T(8,128)S(1)} %slice_select_fusion), channel_id=1, source_target_pairs={{0,3},{3,0},{4,7},{7,4},{8,11},{11,8},{12,15},{15,12},{16,19},{19,... | collective-permute-start | bytes 786440 | tf_op jit(solution)/shard_map/ppermute | solution.py:363
  5.4 4.0 %collective-permute-done = f32[8,2,32,128]{3,2,1,0:T(8,128)S(1)} collective-permute-done((f32[8,2,32,128]{3,2,1,0:T(8,128)S(1)}, f32[8,2,32,128]{3,2,1,0:T(8,128)S(1)}, u32[]{:S(2)}, u32[]{:S(2)}) %collective-permute-start) | collective-permute-done | bytes 262176 | tf_op jit(solution)/shard_map/ppermute | solution.py:363
  9.4 3.3 %pad_maximum_fusion = f32[8,18,32,128]{3,2,1,0:T(8,128)} fusion(f32[8,2,32,128]{3,2,1,0:T(8,128)S(1)} %collective-permute-done, f32[8,16,32,128]{3,2,1,0:T(8,128)} %param.3), kind=kLoop, calls=%fused_computation.1 | loop fusion | flops 589824 | bytes 4718592 | tf_op jit(solution)/shard_map/concatenate | solution.py:368
  12.7 6.6 %all-to-all-start = ((f32[144,32,128]{2,1,0:T(8,128)}), f32[144,32,128]{2,1,0:T(8,128)S(1)}, u32[]{:S(2)}, u32[]{:S(2)}) async-start(f32[144,32,128]{2,1,0:T(8,128)} %bitcast.85), calls=%async_computation | async-start | bytes 4718592 | tf_op jit(solution)/shard_map/all_to_all | solution.py:370
  20.0 0.0 copy-done
  20.0 0.7 gather_fusion
  20.7 0.5 and_select_fusion.shifts
  21.2 45.1 %all-to-all-done = f32[144,32,128]{2,1,0:T(8,128)S(1)} async-done(((f32[144,32,128]{2,1,0:T(8,128)}), f32[144,32,128]{2,1,0:T(8,128)S(1)}, u32[]{:S(2)}, u32[]{:S(2)}) %all-to-all-start) | async-done | bytes 2359328 | tf_op jit(solution)/shard_map/all_to_all | solution.py:370
  66.4 1.7 copy.5
  68.1 11.3 %turn.1 = f32[18,8,36,128]{3,2,1,0:T(8,128)} custom-call(s32[18]{0:T(128)} %and_select_fusion.shifts, f32[18,256,128]{2,1,0:T(8,128)} %bitcast.86), custom_call_target="tpu_custom_call" | custom-call | tf_op jit(solution)/shard_map/turn/pallas_call | solution.py:338
  79.4 2.0 copy.6
  81.5 68.5 %all_to_all.33 = f32[18,8,36,128]{3,2,0,1:T(8,128)S(1)} all-to-all(f32[18,8,36,128]{3,2,0,1:T(8,128)S(1)} %copy.6), channel_id=1, replica_groups=mesh['az'=8,'rad'=4] {'az'}, dimensions={1} | all-to-all | bytes 5308416 | tf_op jit(solution)/shard_map/all_to_all | solution.py:377
  150.0 3.1 %collective-permute-start.2 = (f32[8,2,32,128]{3,2,1,0:T(8,128)S(1)}, f32[8,2,32,128]{3,2,1,0:T(8,128)}, u32[]{:S(2)}, u32[]{:S(2)}) collective-permute-start(f32[8,2,32,128]{3,2,1,0:T(8,128)S(1)} %slice.62), channel_id=1, source_target_pairs={{1,0},{2,1},{3,2},{0,3},{5,4},{6,5},{7,6},{4,7},{9,8},{10,9},{11,1... | collective-permute-start | bytes 786440 | tf_op jit(solution)/shard_map/ppermute | solution.py:383
  153.2 3.9 %collective-permute-done.2 = f32[8,2,32,128]{3,2,1,0:T(8,128)} collective-permute-done((f32[8,2,32,128]{3,2,1,0:T(8,128)S(1)}, f32[8,2,32,128]{3,2,1,0:T(8,128)}, u32[]{:S(2)}, u32[]{:S(2)}) %collective-permute-start.2) | collective-permute-done | bytes 262176 | tf_op jit(solution)/shard_map/ppermute | solution.py:383
  157.0 1.0 slice_select_fusion.1
  158.1 2.3 %collective-permute-start.1 = (f32[8,2,32,128]{3,2,1,0:T(8,128)S(1)}, f32[8,2,32,128]{3,2,1,0:T(8,128)}, u32[]{:S(2)}, u32[]{:S(2)}) collective-permute-start(f32[8,2,32,128]{3,2,1,0:T(8,128)S(1)} %get-tuple-element.6), channel_id=1, source_target_pairs={{0,1},{1,2},{2,3},{3,0},{4,5},{5,6},{6,7},{7,4},{8,9},{9,10},{10,1... | collective-permute-start | bytes 786440 | tf_op jit(solution)/shard_map/ppermute | solution.py:382
  160.3 2.9 %add_reduce_fusion = f32[]{:T(128)} fusion(f32[8,16,32,128]{3,2,1,0:T(8,128)} %param.3), kind=kLoop, calls=%fused_computation.38 | loop fusion | flops 3604479 | bytes 2097156 | tf_op jit(solution)/shard_map/reduce_max | solution.py:358
  163.3 38.6 %pmax.7 = f32[]{:T(128)} all-reduce(f32[]{:T(128)} %add_reduce_fusion), channel_id=1, replica_groups=mesh['az'=8,'rad'=4] {'az','rad'}, use_global_device_ids=true, to_apply=%region_1.0 | all-reduce | flops 1 | bytes 8 | tf_op jit(solution)/shard_map/pmax | solution.py:358
  202.6 0.0 collective-permute-done.1
  202.6 0.1 slice_select_fusion.2.low
  202.7 18.3 %advance.1 = f32[8,16,32,128]{3,2,1,0:T(8,128)} custom-call(f32[8,18,36,128]{3,2,1,0:T(8,128)S(1)} %bitcast.83, f32[8,2,32,128]{3,2,1,0:T(8,128)S(1)} %slice_select_fusion.2.low, f32[8,2,32,128]{3,2,1,0:T(8,128)S(1)} %get-tuple-element.5.high, f32[1]{0:T(128)} %bitcast.19.step), custom_call_target="tpu_custom_call" | custom-call | tf_op jit(solution)/shard_map/advance/pallas_call | solution.py:308
  (3 shorter events, 0.1 us)
Async XLA Ops:
  0.0 20.0 %copy-start = (s32[64]{0:T(128)S(1)}, s32[64]{0:T(128)}, u32[]{:S(2)}) copy-start(s32[64]{0:T(128)} %param.4) | copy-start | bytes 772
  1.1 8.4 %collective-permute-start = (f32[8,2,32,128]{3,2,1,0:T(8,128)S(1)}, f32[8,2,32,128]{3,2,1,0:T(8,128)S(1)}, u32[]{:S(2)}, u32[]{:S(2)}) collective-permute-start(f32[8,2,32,128]{3,2,1,0:T(8,128)S(1)} %slice_select_fusion), channel_id=1, source_target_pairs={{0,3},{3,0},{4,7},{7,4},{8,11},{11,8},{12,15},{15,12},{16,19},{19,... | collective-permute-start | bytes 786440 | tf_op jit(solution)/shard_map/ppermute | solution.py:363
  12.7 53.7 %all-to-all-start = ((f32[144,32,128]{2,1,0:T(8,128)}), f32[144,32,128]{2,1,0:T(8,128)S(1)}, u32[]{:S(2)}, u32[]{:S(2)}) async-start(f32[144,32,128]{2,1,0:T(8,128)} %bitcast.85), calls=%async_computation | async-start | bytes 4718592 | tf_op jit(solution)/shard_map/all_to_all | solution.py:370
  150.0 7.0 %collective-permute-start.2 = (f32[8,2,32,128]{3,2,1,0:T(8,128)S(1)}, f32[8,2,32,128]{3,2,1,0:T(8,128)}, u32[]{:S(2)}, u32[]{:S(2)}) collective-permute-start(f32[8,2,32,128]{3,2,1,0:T(8,128)S(1)} %slice.62), channel_id=1, source_target_pairs={{1,0},{2,1},{3,2},{0,3},{5,4},{6,5},{7,6},{4,7},{9,8},{10,9},{11,1... | collective-permute-start | bytes 786440 | tf_op jit(solution)/shard_map/ppermute | solution.py:383
  158.1 44.5 %collective-permute-start.1 = (f32[8,2,32,128]{3,2,1,0:T(8,128)S(1)}, f32[8,2,32,128]{3,2,1,0:T(8,128)}, u32[]{:S(2)}, u32[]{:S(2)}) collective-permute-start(f32[8,2,32,128]{3,2,1,0:T(8,128)S(1)} %get-tuple-element.6), channel_id=1, source_target_pairs={{0,1},{1,2},{2,3},{3,0},{4,5},{5,6},{6,7},{7,4},{8,9},{9,10},{10,1... | collective-permute-start | bytes 786440 | tf_op jit(solution)/shard_map/ppermute | solution.py:382

commit v3 on v2

--- a/solution.py
+++ b/solution.py
@@ -219,11 +219,11 @@
     return face_flux([pair[0] for pair in pairs], [pair[1] for pair in pairs])
 
 
-def flux_kernel(landed, low, high, step, out, prims, radial_flux, ring_flux):
+def flux_kernel(landed, low, high, peaks, out, prims, radial_flux, ring_flux):
     rows, cells = out.shape[1], out.shape[2]
     depth = out.shape[3]
     chunks = cells // 8
-    dt = step[0]
+    dt = CFL_NUMBER / jnp.max(peaks[...])
 
     def fill(i, _):
         values = primitive([landed[f, i] for f in range(8)])
@@ -236,7 +236,7 @@
         for ref, row in ((low, g), (high, rows + 2 + g)):
             values = primitive([ref[f, g] for f in range(8)])
             for f in range(8):
-                prims[f, row, MARGIN : MARGIN + cells] = values[f]
+                prims[f, row, MARGIN - 2 : MARGIN + cells + 2] = values[f]
 
     def radial(row, q):
         columns = slice(MARGIN + 8 * q, MARGIN + 8 * q + 8)
@@ -302,13 +302,13 @@
     lax.fori_loop(0, rows, advance_row, 0)
 
 
-def advanced(landed, low, high, time_step, rows, cells):
+def advanced(landed, low, high, peaks, rows, cells):
     parts, depth = landed.shape[0], landed.shape[3]
     vmem = pl.BlockSpec(memory_space=pltpu.VMEM)
     return pl.pallas_call(
         flux_kernel,
         out_shape=jax.ShapeDtypeStruct((parts, rows, cells, depth), jnp.float32),
-        in_specs=[vmem, vmem, vmem, pl.BlockSpec(memory_space=pltpu.SMEM)],
+        in_specs=[vmem] * 4,
         out_specs=vmem,
         scratch_shapes=[
             pltpu.VMEM((parts, rows + 4, cells + 3 * MARGIN, depth), jnp.float32),
@@ -317,73 +317,262 @@
         ],
         compiler_params=pltpu.CompilerParams(vmem_limit_bytes=40 * 1024 * 1024),
         name="advance",
-    )(landed, low, high, time_step.reshape(1))
-
-
-def turn_kernel(count, shifts, ring, out, doubled):
-    loop_cells = ring.shape[1]
-    cells = loop_cells // count
-    width = out.shape[2]
-    doubled[:loop_cells] = ring[0]
-    doubled[loop_cells : loop_cells + width] = ring[0, :width]
-    shift = shifts[pl.program_id(0)]
-    for t in range(count):
-        start = lax.rem(t * cells - 2 - shift + 4 * loop_cells, loop_cells)
-        out[0, t] = doubled[pl.ds(start, width)]
-
-
-def turned(rings, shift, count):
-    share, loop_cells, depth = rings.shape
-    width = loop_cells // count + 4
-    return pl.pallas_call(
-        functools.partial(turn_kernel, count),
-        out_shape=jax.ShapeDtypeStruct((share, count, width, depth), jnp.float32),
-        grid_spec=pltpu.PrefetchScalarGridSpec(
-            num_scalar_prefetch=1,
-            grid=(share,),
-            in_specs=[pl.BlockSpec((1, loop_cells, depth), lambda u, s: (u, 0, 0))],
-            out_specs=pl.BlockSpec((1, count, width, depth), lambda u, s: (u, 0, 0, 0)),
-            scratch_shapes=[pltpu.VMEM((loop_cells + width + 4, depth), jnp.float32)],
+    )(landed, low, high, peaks)
+
+
+CHUNKS = 4
+
+
+def exchange_kernel(
+    rows, az_count, rad_count,
+    fields, offsets, shear,
+    landed, low, high, rad_peaks,
+    ghosts, windows, ghost_send, ghost_land, low_send, high_send, low_land, high_land, az_peaks,
+    *rest,
+):
+    rings = rest[: CHUNKS + 1]
+    out_send, out_recv, back_send, back_recv, rad_send, rad_recv, peak_send, peak_recv = rest[
+        CHUNKS + 1 : CHUNKS + 9
+    ]
+    barrier = pltpu.get_barrier_semaphore()
+    az = lax.axis_index("az")
+    rad = lax.axis_index("rad")
+    cells = fields.shape[1]
+    width = landed.shape[1]
+    loop_cells = cells * az_count
+    radial_cells = rows * rad_count
+    parts = fields.shape[0] // rows
+    main = fields.shape[0] // az_count
+    spare = 2 * parts // az_count
+    piece = main // CHUNKS
+    lowest = rad == 0
+    highest = rad == rad_count - 1
+
+    def az_peer(k):
+        return lax.rem(az + k, az_count)
+
+    def rad_peer(k):
+        return lax.rem(rad + k, rad_count)
+
+    for k in range(1, az_count):
+        pl.semaphore_signal(
+            barrier, inc=1, device_id=(az_peer(k), rad), device_id_type=pl.DeviceIdType.MESH
+        )
+    for k in range(1, rad_count):
+        pl.semaphore_signal(
+            barrier, inc=1, device_id=(az, rad_peer(k)), device_id_type=pl.DeviceIdType.MESH
+        )
+    pl.semaphore_wait(barrier, az_count + rad_count - 2)
+
+    def remote(src, dst, send, recv, target):
+        return pltpu.make_async_remote_copy(
+            src_ref=src,
+            dst_ref=dst,
+            send_sem=send,
+            recv_sem=recv,
+            device_id=target,
+            device_id_type=pl.DeviceIdType.MESH,
+        )
+
+    for f in range(parts):
+        for g in range(2):
+            edge = jnp.where(lowest, g, rows - 2 + g)
+            ghost_send[2 * f + g] = fields[f * rows + edge]
+    ghost_copy = remote(
+        ghost_send, ghost_land, rad_send.at[0], rad_recv.at[0], (az, rad_count - 1 - rad)
+    )
+    ghost_copy.start()
+
+    own = pl.ds(pl.multiple_of(az * cells, cells), cells)
+
+    def outward(c, k):
+        peer = az_peer(k)
+        if c < CHUNKS:
+            src = fields.at[pl.ds(peer * main + c * piece, piece)]
+        else:
+            src = ghost_land.at[pl.ds(peer * spare, spare)]
+        return remote(
+            src, rings[c].at[:, own], out_send.at[c, k], out_recv.at[c, k], (peer, rad)
+        )
+
+    sends = []
+    for c in range(CHUNKS):
+        for k in range(1, az_count):
+            sends.append(outward(c, k))
+            sends[-1].start()
+    ghost_copy.wait()
+    for k in range(1, az_count):
+        sends.append(outward(CHUNKS, k))
+        sends[-1].start()
+    for c in range(CHUNKS):
+        rings[c][:, own] = fields[pl.ds(az * main + c * piece, piece)]
+    rings[CHUNKS][:, own] = ghost_land[pl.ds(az * spare, spare)]
+
+    def peak_of(i, best):
+        return jnp.maximum(
+            best, cell_speed(primitive([fields[f * rows + i] for f in range(parts)]))
+        )
+
+    best = lax.fori_loop(0, rows, peak_of, jnp.zeros(fields.shape[1:], jnp.float32))
+    tile = best[:8]
+    for q in range(1, cells // 8):
+        tile = jnp.maximum(tile, best[8 * q : 8 * q + 8])
+    az_peaks[az] = tile
+    peak_copies = []
+    for k in range(1, az_count):
+        peak_copies.append(
+            remote(
+                az_peaks.at[az],
+                az_peaks.at[az],
+                peak_send.at[k],
+                peak_recv.at[k],
+                (az_peer(k), rad),
+            )
+        )
+        peak_copies[-1].start()
+
+    returns = []
+
+    def backward(first, count, place, c, k):
+        peer = az_peer(k)
+        return remote(
+            windows.at[peer, pl.ds(first, count)],
+            place,
+            back_send.at[c, k],
+            back_recv.at[c, k],
+            (peer, rad),
+        )
+
+    for c in range(CHUNKS + 1):
+        for k in range(1, az_count):
+            outward(c, k).wait_recv()
+        count = piece if c < CHUNKS else spare
+        first = c * piece
+        ring = rings[c]
+        for u in range(count):
+            ring[u, loop_cells : loop_cells + width + 4] = ring[u, : width + 4]
+        for u in range(count):
+            if c < CHUNKS:
+                row = rad * rows + lax.rem(az * main + first + u, rows)
+                shift = offsets[row]
+            else:
+                g = lax.rem(az * spare + u, 2)
+                row = jnp.where(lowest, radial_cells - 2, 0) + g
+                shift = offsets[row] + jnp.where(lowest, shear[0], -shear[0])
+            for t in range(az_count):
+                start = lax.rem(t * cells - 2 - shift + 4 * loop_cells, loop_cells)
+                windows[t, first + u] = ring[u, pl.ds(start, width)]
+        if c < CHUNKS:
+            place = landed.at[pl.ds(az * main + first, count)]
+        else:
+            place = ghosts.at[pl.ds(az * spare, count)]
+        for k in range(1, az_count):
+            returns.append(backward(first, count, place, c, k))
+            returns[-1].start()
+        if c < CHUNKS:
+            landed[pl.ds(az * main + first, count)] = windows[az, first : first + count]
+        else:
+            ghosts[pl.ds(az * spare, count)] = windows[az, first : first + count]
+
+    for copy in peak_copies:
+        copy.wait_recv()
+    tile = az_peaks[0]
+    for a in range(1, az_count):
+        tile = jnp.maximum(tile, az_peaks[a])
+    rad_peaks[rad] = tile
+    for k in range(1, rad_count):
+        copy = remote(
+            rad_peaks.at[rad],
+            rad_peaks.at[rad],
+            peak_send.at[az_count + k],
+            peak_recv.at[az_count + k],
+            (az, rad_peer(k)),
+        )
+        peak_copies.append(copy)
+        copy.start()
+
+    for copy in returns:
+        copy.wait_recv()
+    for f in range(parts):
+        for g in range(2):
+            low_send[2 * f + g] = landed[f * rows + rows - 2 + g]
+            high_send[2 * f + g] = landed[f * rows + g]
+    up = remote(low_send, low_land, rad_send.at[1], rad_recv.at[1], (az, rad_peer(1)))
+    down = remote(
+        high_send, high_land, rad_send.at[2], rad_recv.at[2], (az, rad_peer(rad_count - 1))
+    )
+    up.start()
+    down.start()
+    for copy in sends + returns:
+        copy.wait_send()
+    for copy in peak_copies:
+        copy.wait_send()
+    for copy in peak_copies[az_count - 1 :]:
+        copy.wait_recv()
+    up.wait()
+    down.wait()
+    low[...] = jnp.where(lowest, ghosts[...], low_land[...])
+    high[...] = jnp.where(highest, ghosts[...], high_land[...])
+
+
+def exchanged(fields, offsets, boundary_shift):
+    parts, rows, cells, depth = fields.shape
+    az_count = lax.axis_size("az")
+    rad_count = lax.axis_size("rad")
+    width = cells + 4
+    main = parts * rows // az_count
+    spare = 2 * parts // az_count
+    ring_cells = cells * az_count + width + 4
+    vmem = pl.BlockSpec(memory_space=pltpu.VMEM)
+    smem = pl.BlockSpec(memory_space=pltpu.SMEM)
+
+    def buffer(*shape):
+        return pltpu.VMEM((*shape, depth), jnp.float32)
+
+    edge = jax.ShapeDtypeStruct((2 * parts, width, depth), jnp.float32)
+    landed, low, high, peaks = pl.pallas_call(
+        functools.partial(exchange_kernel, rows, az_count, rad_count),
+        out_shape=[
+            jax.ShapeDtypeStruct((parts * rows, width, depth), jnp.float32),
+            edge,
+            edge,
+            jax.ShapeDtypeStruct((rad_count, 8, depth), jnp.float32),
+        ],
+        in_specs=[vmem, smem, smem],
+        out_specs=[vmem] * 4,
+        scratch_shapes=[
+            buffer(2 * parts, width),
+            buffer(az_count, main + spare, width),
+            buffer(2 * parts, cells),
+            buffer(2 * parts, cells),
+            buffer(2 * parts, width),
+            buffer(2 * parts, width),
+            buffer(2 * parts, width),
+            buffer(2 * parts, width),
+            buffer(az_count, 8),
+        ]
+        + [buffer(main // CHUNKS, ring_cells)] * CHUNKS
+        + [buffer(spare, ring_cells)]
+        + [pltpu.SemaphoreType.DMA((CHUNKS + 1, az_count))] * 4
+        + [pltpu.SemaphoreType.DMA((3,))] * 2
+        + [pltpu.SemaphoreType.DMA((az_count + rad_count,))] * 2,
+        compiler_params=pltpu.CompilerParams(
+            collective_id=0, has_side_effects=True, vmem_limit_bytes=40 * 1024 * 1024
         ),
-        name="turn",
-    )(shift, rings)
+        name="exchange",
+    )(fields.reshape(parts * rows, cells, depth), offsets, boundary_shift)
+    return (
+        landed.reshape(parts, rows, width, depth),
+        low.reshape(parts, 2, width, depth),
+        high.reshape(parts, 2, width, depth),
+        peaks,
+    )
 
 
 def local(fields, offsets, boundary_shift):
-    parts, rows, cells, depth = fields.shape
-    azimuth_devices = lax.axis_size("az")
-    radial_devices = lax.axis_size("rad")
-    loop_cells = cells * azimuth_devices
-    radial_cells = rows * radial_devices
-    time_step = CFL_NUMBER / lax.pmax(jnp.max(cell_speed(primitive(fields))), ("az", "rad"))
-    radial_index = lax.axis_index("rad")
-    lowest = radial_index == 0
-    highest = radial_index == radial_devices - 1
-    shear_cells = boundary_shift[0]
-    ghost = lax.ppermute(
-        jnp.where(lowest, fields[:, :2], fields[:, rows - 2 :]),
-        "rad",
-        [(0, radial_devices - 1), (radial_devices - 1, 0)],
-    )
-    units = jnp.concatenate([fields, ghost], axis=1).reshape(parts * (rows + 2), cells, depth)
-    share = units.shape[0] // azimuth_devices
-    rings = lax.all_to_all(units, "az", 0, 1, tiled=True)
-    slot = jnp.mod(lax.axis_index("az") * share + jnp.arange(share, dtype=jnp.int32), rows + 2)
-    ghost_row = jnp.where(lowest, radial_cells - 2, 0) + slot - rows
-    row = jnp.where(slot < rows, radial_index * rows + slot, ghost_row)
-    extra = jnp.where(slot < rows, 0, jnp.where(lowest, shear_cells, -shear_cells))
-    shift = jnp.take(offsets, row) + extra
-    windows = turned(rings, jnp.mod(shift, loop_cells), azimuth_devices)
-    landed = lax.all_to_all(windows, "az", 1, 0, tiled=True)
-    landed = landed.reshape(parts, rows + 2, cells + 4, depth)
-    forward = [(i, (i + 1) % radial_devices) for i in range(radial_devices)]
-    backward = [(target, source) for source, target in forward]
-    spare = landed[:, rows:, 2 : cells + 2]
-    low = lax.ppermute(landed[:, rows - 2 : rows, 2 : cells + 2], "rad", forward)
-    high = lax.ppermute(landed[:, :2, 2 : cells + 2], "rad", backward)
-    low = jnp.where(lowest, spare, low)
-    high = jnp.where(highest, spare, high)
-    return advanced(landed, low, high, time_step, rows, cells)
+    rows, cells = fields.shape[1:3]
+    landed, low, high, peaks = exchanged(fields, offsets, boundary_shift)
+    return advanced(landed, low, high, peaks, rows, cells)
 
 
 def solution(mesh):

time: 222 us -> 145 us (0.65)
  Pallas kernels: 29.6 us -> 141 us
  blocking collectives: 107 us -> 0 us
  waiting for transfers between devices: 53.1 us -> 0 us
  starting transfers between devices: 16.3 us -> 0 us
  other arithmetic: 8.96 us -> 0 us
    pallas_call x1, Pallas kernels: 11.3 us -> 123 us  [exchanged(): pl.pallas_call(functools.partial(exchange_kernel, rows, az_count, rad_cou...]
    all_to_all x1 -> x0, blocking collectives: 68.5 us -> none  [local(): landed = lax.all_to_all(windows, 'az', 1, 0, tiled=True)]
    all_to_all x1 -> x0, waiting for transfers between devices: 45.1 us -> none  [local(): rings = lax.all_to_all(units, 'az', 0, 1, tiled=True)]
    pmax x1 -> x0, blocking collectives: 38.6 us -> none  [local(): lax.pmax(jnp.max(cell_speed(primitive(fields))), ('az', 'rad'))]
    ppermute x3 -> x0, starting transfers between devices: 9.71 us -> none  [the longest x1 4.31 us: local(): lax.ppermute(jnp.where(lowest, fields[:, :2], fields[:, rows - 2:]), 'rad...]
    ppermute x3 -> x0, waiting for transfers between devices: 7.93 us -> none  [the longest x1 4.04 us: local(): lax.ppermute(jnp.where(lowest, fields[:, :2], fields[:, rows - 2:]), 'rad...]
    all_to_all x1 -> x0, starting transfers between devices: 6.58 us -> none  [local(): rings = lax.all_to_all(units, 'az', 0, 1, tiled=True)]
    concatenate x1 -> x0, other arithmetic: 3.27 us -> none  [local(): jnp.concatenate([fields, ghost], axis=1)]
  transfers between devices with their start and end apart: 4 -> 0, of which waited for: 3 -> 0; matrix products, arithmetic and copies ran while one was open for 2% -> 0% of each run, Pallas kernels for 0% -> 0%
where the time goes in v3:
time: 145 us; the launch traced here: 144 us
  Pallas kernels  141 us (97%)
  local copies, waits for them, and re-layouts  2.24 us (2%)
    pallas_call x1, Pallas kernels, exchanged(): pl.pallas_call(functools.partial(exchange_kernel, rows, az_count, rad_cou...  123 us
    pallas_call x1, Pallas kernels, advanced(): pl.pallas_call(flux_kernel, out_shape=jax.ShapeDtypeStruct((parts, rows,...  18.4 us

profile of v3, /device:TPU:0, one launch (start us, length us, event | category | flops | bytes accessed | tf_op | source)
XLA Modules:
  0.0 143.9 jit_solution(13027648217974212942)
XLA Ops:
  0.7 0.0 copy-start
  0.7 1.6 %copy-done = f32[8,16,32,128]{3,2,1,0:T(8,128)S(1)} copy-done((f32[8,16,32,128]{3,2,1,0:T(8,128)S(1)}, f32[8,16,32,128]{3,2,1,0:T(8,128)}, u32[]{:S(2)}) %copy-start) | copy-done | bytes 2097176
  2.2 0.0 copy-start.1
  2.2 0.7 copy-done.1
  2.9 122.6 %exchange.1 = (f32[128,36,128]{2,1,0:T(8,128)S(1)}, f32[16,36,128]{2,1,0:T(8,128)S(1)}, f32[16,36,128]{2,1,0:T(8,128)S(1)}, f32[4,8,128]{2,1,0:T(8,128)S(1)}) custom-call(f32[128,32,128]{2,1,0:T(8,128)S(1)} %bitcast.5, s32[64]{0:T(128)S(1)} %copy-done.1, s32[1]{0:T(128)S(6)} %copy.4.shear), custom_call_target="tpu_custom_call" | custom-call | tf_op jit(solution)/shard_map/exchange/pallas_call | solution.py:533
  125.5 18.4 %advance.1 = f32[8,16,32,128]{3,2,1,0:T(8,128)} custom-call(f32[8,16,36,128]{3,2,1,0:T(8,128)S(1)} %bitcast.4, f32[8,2,36,128]{3,2,1,0:T(8,128)S(1)} %bitcast.6, f32[8,2,36,128]{3,2,1,0:T(8,128)S(1)} %bitcast.7, f32[4,8,128]{2,1,0:T(8,128)S(1)} %get-tuple-element.12.peaks), custom_call_target="tpu_custom_call" | custom-call | tf_op jit(solution)/shard_map/advance/pallas_call | solution.py:308
Async XLA Ops:
  0.7 1.6 %copy-start = (f32[8,16,32,128]{3,2,1,0:T(8,128)S(1)}, f32[8,16,32,128]{3,2,1,0:T(8,128)}, u32[]{:S(2)}) copy-start(f32[8,16,32,128]{3,2,1,0:T(8,128)} %param.3) | copy-start | bytes 6291460
  2.2 0.7 copy-start.1

commit v4 on v3

--- a/solution.py
+++ b/solution.py
@@ -223,10 +223,11 @@
     rows, cells = out.shape[1], out.shape[2]
     depth = out.shape[3]
     chunks = cells // 8
+    width = cells + 4
     dt = CFL_NUMBER / jnp.max(peaks[...])
 
     def fill(i, _):
-        values = primitive([landed[f, i] for f in range(8)])
+        values = primitive([landed[pl.ds((f * rows + i) * width, width)] for f in range(8)])
         for f in range(8):
             prims[f, i + 2, MARGIN - 2 : MARGIN + cells + 2] = values[f]
         return 0
@@ -286,7 +287,7 @@
                 rights.append(pltpu.roll(here - slope, depth - 1, 1))
             above = face_flux(lefts, rights)
             gather(ORDERS[2], [value - pltpu.roll(value, 1, 1) for value in above])
-            state = [landed[f, i, 8 * q + 2 : 8 * q + 10] for f in range(8)]
+            state = [landed[pl.ds((f * rows + i) * width + 8 * q + 2, 8)] for f in range(8)]
             speed_x = prims[1, row, columns]
             gains = {
                 1: (2.0 * OMEGA_RATE) * state[2],
@@ -303,7 +304,7 @@
 
 
 def advanced(landed, low, high, peaks, rows, cells):
-    parts, depth = landed.shape[0], landed.shape[3]
+    parts, depth = low.shape[0], low.shape[3]
     vmem = pl.BlockSpec(memory_space=pltpu.VMEM)
     return pl.pallas_call(
         flux_kernel,
@@ -327,7 +328,7 @@
     rows, az_count, rad_count,
     fields, offsets, shear,
     landed, low, high, rad_peaks,
-    ghosts, windows, ghost_send, ghost_land, low_send, high_send, low_land, high_land, az_peaks,
+    ghosts, windows, ghost_windows, ghost_send, ghost_land, low_send, high_send, low_land, high_land, az_peaks,
     *rest,
 ):
     rings = rest[: CHUNKS + 1]
@@ -338,13 +339,15 @@
     az = lax.axis_index("az")
     rad = lax.axis_index("rad")
     cells = fields.shape[1]
-    width = landed.shape[1]
+    width = low.shape[1]
     loop_cells = cells * az_count
     radial_cells = rows * rad_count
     parts = fields.shape[0] // rows
-    main = fields.shape[0] // az_count
     spare = 2 * parts // az_count
-    piece = main // CHUNKS
+    band = rows // CHUNKS
+    piece = parts * band // az_count
+    peers = sorted(range(1, az_count), key=lambda k: -min(k, az_count - k))
+    order = [0, CHUNKS - 1, CHUNKS, *range(1, CHUNKS - 1)]
     lowest = rad == 0
     highest = rad == rad_count - 1
 
@@ -374,6 +377,13 @@
             device_id_type=pl.DeviceIdType.MESH,
         )
 
+    def unit(device, c):
+        flat = device * piece
+        return lax.div(flat, band) * rows + c * band + lax.rem(flat, band)
+
+    def packed(start, count):
+        return pl.ds(pl.multiple_of(start * width, 8), count * width)
+
     for f in range(parts):
         for g in range(2):
             edge = jnp.where(lowest, g, rows - 2 + g)
@@ -388,7 +398,7 @@
     def outward(c, k):
         peer = az_peer(k)
         if c < CHUNKS:
-            src = fields.at[pl.ds(peer * main + c * piece, piece)]
+            src = fields.at[pl.ds(unit(peer, c), piece)]
         else:
             src = ghost_land.at[pl.ds(peer * spare, spare)]
         return remote(
@@ -396,17 +406,15 @@
         )
 
     sends = []
-    for c in range(CHUNKS):
-        for k in range(1, az_count):
+    for c in order:
+        if c == CHUNKS:
+            ghost_copy.wait()
+            rings[c][:, own] = ghost_land[pl.ds(az * spare, spare)]
+        else:
+            rings[c][:, own] = fields[pl.ds(unit(az, c), piece)]
+        for k in peers:
             sends.append(outward(c, k))
             sends[-1].start()
-    ghost_copy.wait()
-    for k in range(1, az_count):
-        sends.append(outward(CHUNKS, k))
-        sends[-1].start()
-    for c in range(CHUNKS):
-        rings[c][:, own] = fields[pl.ds(az * main + c * piece, piece)]
-    rings[CHUNKS][:, own] = ghost_land[pl.ds(az * spare, spare)]
 
     def peak_of(i, best):
         return jnp.maximum(
@@ -433,27 +441,41 @@
 
     returns = []
 
-    def backward(first, count, place, c, k):
+    def backward(c, k):
         peer = az_peer(k)
-        return remote(
-            windows.at[peer, pl.ds(first, count)],
-            place,
-            back_send.at[c, k],
-            back_recv.at[c, k],
-            (peer, rad),
-        )
-
-    for c in range(CHUNKS + 1):
-        for k in range(1, az_count):
+        if c < CHUNKS:
+            source = windows.at[peer, c * piece * width : (c + 1) * piece * width]
+            place = landed.at[packed(unit(az, c), piece)]
+        else:
+            source = ghost_windows.at[peer]
+            place = ghosts.at[pl.ds(az * spare, spare)]
+        return remote(source, place, back_send.at[c, k], back_recv.at[c, k], (peer, rad))
+
+    def edges_out(c, source, send, land, slot, step):
+        begin = 0 if c == 0 else rows - 2
+        for f in range(parts):
+            for g in range(2):
+                at = (f * rows + begin + g) * width
+                send[2 * f + g] = source[at : at + width]
+        copy = remote(send, land, rad_send.at[slot], rad_recv.at[slot], (az, rad_peer(step)))
+        copy.start()
+        return copy
+
+    def collect(c):
+        for copy, chunk in returns:
+            if chunk == c:
+                copy.wait_recv()
+
+    for c in order:
+        for k in peers:
             outward(c, k).wait_recv()
         count = piece if c < CHUNKS else spare
-        first = c * piece
         ring = rings[c]
         for u in range(count):
             ring[u, loop_cells : loop_cells + width + 4] = ring[u, : width + 4]
         for u in range(count):
             if c < CHUNKS:
-                row = rad * rows + lax.rem(az * main + first + u, rows)
+                row = rad * rows + lax.rem(unit(az, c), rows) + u
                 shift = offsets[row]
             else:
                 g = lax.rem(az * spare + u, 2)
@@ -461,18 +483,22 @@
                 shift = offsets[row] + jnp.where(lowest, shear[0], -shear[0])
             for t in range(az_count):
                 start = lax.rem(t * cells - 2 - shift + 4 * loop_cells, loop_cells)
-                windows[t, first + u] = ring[u, pl.ds(start, width)]
+                window = ring[u, pl.ds(start, width)]
+                if c < CHUNKS:
+                    at = (c * piece + u) * width
+                    windows[t, at : at + width] = window
+                else:
+                    ghost_windows[t, u] = window
+        for k in peers:
+            copy = backward(c, k)
+            copy.start()
+            returns.append((copy, c))
         if c < CHUNKS:
-            place = landed.at[pl.ds(az * main + first, count)]
+            landed[packed(unit(az, c), piece)] = windows[
+                az, c * piece * width : (c + 1) * piece * width
+            ]
         else:
-            place = ghosts.at[pl.ds(az * spare, count)]
-        for k in range(1, az_count):
-            returns.append(backward(first, count, place, c, k))
-            returns[-1].start()
-        if c < CHUNKS:
-            landed[pl.ds(az * main + first, count)] = windows[az, first : first + count]
-        else:
-            ghosts[pl.ds(az * spare, count)] = windows[az, first : first + count]
+            ghosts[pl.ds(az * spare, spare)] = ghost_windows[az]
 
     for copy in peak_copies:
         copy.wait_recv()
@@ -491,28 +517,23 @@
         peak_copies.append(copy)
         copy.start()
 
-    for copy in returns:
-        copy.wait_recv()
-    for f in range(parts):
-        for g in range(2):
-            low_send[2 * f + g] = landed[f * rows + rows - 2 + g]
-            high_send[2 * f + g] = landed[f * rows + g]
-    up = remote(low_send, low_land, rad_send.at[1], rad_recv.at[1], (az, rad_peer(1)))
-    down = remote(
-        high_send, high_land, rad_send.at[2], rad_recv.at[2], (az, rad_peer(rad_count - 1))
-    )
-    up.start()
-    down.start()
-    for copy in sends + returns:
-        copy.wait_send()
-    for copy in peak_copies:
-        copy.wait_send()
+    collect(0)
+    down = edges_out(0, landed, high_send, high_land, 2, rad_count - 1)
+    collect(CHUNKS - 1)
+    up = edges_out(CHUNKS - 1, landed, low_send, low_land, 1, 1)
+    collect(CHUNKS)
     for copy in peak_copies[az_count - 1 :]:
         copy.wait_recv()
+    for copy in sends + peak_copies:
+        copy.wait_send()
     up.wait()
     down.wait()
     low[...] = jnp.where(lowest, ghosts[...], low_land[...])
     high[...] = jnp.where(highest, ghosts[...], high_land[...])
+    for c in range(1, CHUNKS - 1):
+        collect(c)
+    for copy, _ in returns:
+        copy.wait_send()
 
 
 def exchanged(fields, offsets, boundary_shift):
@@ -520,7 +541,7 @@
     az_count = lax.axis_size("az")
     rad_count = lax.axis_size("rad")
     width = cells + 4
-    main = parts * rows // az_count
+    piece = parts * rows // CHUNKS // az_count
     spare = 2 * parts // az_count
     ring_cells = cells * az_count + width + 4
     vmem = pl.BlockSpec(memory_space=pltpu.VMEM)
@@ -533,7 +554,7 @@
     landed, low, high, peaks = pl.pallas_call(
         functools.partial(exchange_kernel, rows, az_count, rad_count),
         out_shape=[
-            jax.ShapeDtypeStruct((parts * rows, width, depth), jnp.float32),
+            jax.ShapeDtypeStruct((parts * rows * width, depth), jnp.float32),
             edge,
             edge,
             jax.ShapeDtypeStruct((rad_count, 8, depth), jnp.float32),
@@ -542,7 +563,8 @@
         out_specs=[vmem] * 4,
         scratch_shapes=[
             buffer(2 * parts, width),
-            buffer(az_count, main + spare, width),
+            buffer(az_count, CHUNKS * piece * width),
+            buffer(az_count, spare, width),
             buffer(2 * parts, cells),
             buffer(2 * parts, cells),
             buffer(2 * parts, width),
@@ -551,7 +573,7 @@
             buffer(2 * parts, width),
             buffer(az_count, 8),
         ]
-        + [buffer(main // CHUNKS, ring_cells)] * CHUNKS
+        + [buffer(piece, ring_cells)] * CHUNKS
         + [buffer(spare, ring_cells)]
         + [pltpu.SemaphoreType.DMA((CHUNKS + 1, az_count))] * 4
         + [pltpu.SemaphoreType.DMA((3,))] * 2
@@ -562,7 +584,7 @@
         name="exchange",
     )(fields.reshape(parts * rows, cells, depth), offsets, boundary_shift)
     return (
-        landed.reshape(parts, rows, width, depth),
+        landed,
         low.reshape(parts, 2, width, depth),
         high.reshape(parts, 2, width, depth),
         peaks,

time: 145 us -> 137 us (0.945)
  Pallas kernels: 141 us -> 134 us
    pallas_call x1, Pallas kernels: 123 us -> 116 us  [exchanged(): pl.pallas_call(functools.partial(exchange_kernel, rows, az_count, rad_cou...]
where the time goes in v4:
time: 137 us
  Pallas kernels  134 us (98%)
  local copies, waits for them, and re-layouts  2.24 us (2%)
    pallas_call x1, Pallas kernels, exchanged(): pl.pallas_call(functools.partial(exchange_kernel, rows, az_count, rad_cou...  116 us
    pallas_call x1, Pallas kernels, advanced(): pl.pallas_call(flux_kernel, out_shape=jax.ShapeDtypeStruct((parts, rows,...  18.4 us

profile of v4, /device:TPU:0, one launch (start us, length us, event | category | flops | bytes accessed | tf_op | source)
XLA Modules:
  0.0 137.0 jit_solution(16545064798600362510)
XLA Ops:
  0.7 0.0 copy-start
  0.7 1.6 %copy-done = f32[8,16,32,128]{3,2,1,0:T(8,128)S(1)} copy-done((f32[8,16,32,128]{3,2,1,0:T(8,128)S(1)}, f32[8,16,32,128]{3,2,1,0:T(8,128)}, u32[]{:S(2)}) %copy-start) | copy-done | bytes 2097176
  2.2 0.0 copy-start.1
  2.2 0.7 copy-done.1
  2.9 115.6 %exchange.1 = (f32[4608,128]{1,0:T(8,128)S(1)}, f32[16,36,128]{2,1,0:T(8,128)S(1)}, f32[16,36,128]{2,1,0:T(8,128)S(1)}, f32[4,8,128]{2,1,0:T(8,128)S(1)}) custom-call(f32[128,32,128]{2,1,0:T(8,128)S(1)} %bitcast.3, s32[64]{0:T(128)S(1)} %copy-done.1, s32[1]{0:T(128)S(6)} %copy.4.shear), custom_call_target="tpu_custom_call" | custom-call | tf_op jit(solution)/shard_map/exchange/pallas_call | solution.py:554
  118.5 18.4 %advance.1 = f32[8,16,32,128]{3,2,1,0:T(8,128)} custom-call(f32[4608,128]{1,0:T(8,128)S(1)} %get-tuple-element.9.landed, f32[8,2,36,128]{3,2,1,0:T(8,128)S(1)} %bitcast.4, f32[8,2,36,128]{3,2,1,0:T(8,128)S(1)} %bitcast.5, f32[4,8,128]{2,1,0:T(8,128)S(1)} %get-tuple-element.12.peaks), custom_call_target="tpu_custom_call" | custom-call | tf_op jit(solution)/shard_map/advance/pallas_call | solution.py:309
Async XLA Ops:
  0.7 1.6 %copy-start = (f32[8,16,32,128]{3,2,1,0:T(8,128)S(1)}, f32[8,16,32,128]{3,2,1,0:T(8,128)}, u32[]{:S(2)}) copy-start(f32[8,16,32,128]{3,2,1,0:T(8,128)} %param.3) | copy-start | bytes 6291460
  2.2 0.7 copy-start.1

commit v5 on v4

--- a/solution.py
+++ b/solution.py
@@ -347,7 +347,7 @@
     band = rows // CHUNKS
     piece = parts * band // az_count
     peers = sorted(range(1, az_count), key=lambda k: -min(k, az_count - k))
-    order = [0, CHUNKS - 1, CHUNKS, *range(1, CHUNKS - 1)]
+    order = [0, CHUNKS - 1, *range(1, CHUNKS - 1), CHUNKS]
     lowest = rad == 0
     highest = rad == rad_count - 1
 
@@ -521,17 +521,17 @@
     down = edges_out(0, landed, high_send, high_land, 2, rad_count - 1)
     collect(CHUNKS - 1)
     up = edges_out(CHUNKS - 1, landed, low_send, low_land, 1, 1)
-    collect(CHUNKS)
     for copy in peak_copies[az_count - 1 :]:
         copy.wait_recv()
     for copy in sends + peak_copies:
         copy.wait_send()
     up.wait()
     down.wait()
+    for c in range(1, CHUNKS - 1):
+        collect(c)
+    collect(CHUNKS)
     low[...] = jnp.where(lowest, ghosts[...], low_land[...])
     high[...] = jnp.where(highest, ghosts[...], high_land[...])
-    for c in range(1, CHUNKS - 1):
-        collect(c)
     for copy, _ in returns:
         copy.wait_send()
 

time: 137 us -> 139 us (1.015)
  Pallas kernels: 134 us -> 136 us
    pallas_call x1, Pallas kernels: 116 us -> 117 us  [exchanged(): pl.pallas_call(functools.partial(exchange_kernel, rows, az_count, rad_cou...]
where the time goes in v5:
time: 139 us
  Pallas kernels  136 us (98%)
  local copies, waits for them, and re-layouts  2.24 us (2%)
    pallas_call x1, Pallas kernels, exchanged(): pl.pallas_call(functools.partial(exchange_kernel, rows, az_count, rad_cou...  117 us
    pallas_call x1, Pallas kernels, advanced(): pl.pallas_call(flux_kernel, out_shape=jax.ShapeDtypeStruct((parts, rows,...  18.4 us

profile of v5, /device:TPU:0, one launch (start us, length us, event | category | flops | bytes accessed | tf_op | source)
XLA Modules:
  0.0 138.6 jit_solution(17035443319433017168)
XLA Ops:
  0.7 0.0 copy-start
  0.7 1.6 %copy-done = f32[8,16,32,128]{3,2,1,0:T(8,128)S(1)} copy-done((f32[8,16,32,128]{3,2,1,0:T(8,128)S(1)}, f32[8,16,32,128]{3,2,1,0:T(8,128)}, u32[]{:S(2)}) %copy-start) | copy-done | bytes 2097176
  2.2 0.0 copy-start.1
  2.2 0.7 copy-done.1
  2.9 117.3 %exchange.1 = (f32[4608,128]{1,0:T(8,128)S(1)}, f32[16,36,128]{2,1,0:T(8,128)S(1)}, f32[16,36,128]{2,1,0:T(8,128)S(1)}, f32[4,8,128]{2,1,0:T(8,128)S(1)}) custom-call(f32[128,32,128]{2,1,0:T(8,128)S(1)} %bitcast.3, s32[64]{0:T(128)S(1)} %copy-done.1, s32[1]{0:T(128)S(6)} %copy.4.shear), custom_call_target="tpu_custom_call" | custom-call | tf_op jit(solution)/shard_map/exchange/pallas_call | solution.py:554
  120.2 18.4 %advance.1 = f32[8,16,32,128]{3,2,1,0:T(8,128)} custom-call(f32[4608,128]{1,0:T(8,128)S(1)} %get-tuple-element.9.landed, f32[8,2,36,128]{3,2,1,0:T(8,128)S(1)} %bitcast.4, f32[8,2,36,128]{3,2,1,0:T(8,128)S(1)} %bitcast.5, f32[4,8,128]{2,1,0:T(8,128)S(1)} %get-tuple-element.12.peaks), custom_call_target="tpu_custom_call" | custom-call | tf_op jit(solution)/shard_map/advance/pallas_call | solution.py:309
Async XLA Ops:
  0.7 1.6 %copy-start = (f32[8,16,32,128]{3,2,1,0:T(8,128)S(1)}, f32[8,16,32,128]{3,2,1,0:T(8,128)}, u32[]{:S(2)}) copy-start(f32[8,16,32,128]{3,2,1,0:T(8,128)} %param.3) | copy-start | bytes 6291460
  2.2 0.7 copy-start.1
